TPU v7x, 1024 devices: a whole 4x4x32 slice. The times are simulated.
1024 devices in a mesh: box: 64 (over z, core), sub: 16 (over y, x).
Axes of the slice: x: 4, y: 4, z: 32, core: 2. Of those that a mesh axis runs over, the one named last changes fastest.
Arguments:
- source: float32 [256, 512, 256], P('box', 'sub'), may hold values from -8 to 8
- guess: float32 [256, 512, 256], P('box', 'sub'), may hold values from -8 to 8
- mass_coef: float32 [256, 512, 256], P('box', 'sub'), may hold values from 0.05 to 1
- diffusion: float32 [256, 512, 256], P('box', 'sub'), may hold values from 0.25 to 4
Outputs:
- final: float32 [256, 512, 256], P('box', 'sub')
All inputs are finite; a program needn't handle non-finite values.
Results may differ from a plain program's by a relative error of at most 0.00002.
Values sent between devices are 32-bit elements; how exact they have to be, the bound alone decides.
A program may use at most 32 MiB of HBM per device.

v0:
```python
import jax
import jax.numpy as jnp
from jax import lax
from jax.sharding import PartitionSpec as P

CHEB_C = 8


FINE_LOW = 0.25
FINE_HIGH = 2.0
COARSE_LOW = 0.05
COARSE_HIGH = 2.0


def with_halo(block, sides, width):
    for axis, dim in sides:
        count = lax.axis_size(axis)
        forward = [(i, i + 1) for i in range(count - 1)]
        backward = [(target, source) for source, target in forward]
        low = lax.ppermute(
            lax.slice_in_dim(block, block.shape[dim] - width, None, axis=dim), axis, forward
        )
        high = lax.ppermute(lax.slice_in_dim(block, 0, width, axis=dim), axis, backward)
        block = jnp.concatenate([low, block, high], axis=dim)
    return block


def cheb_coeffs(count_steps, low_end, high_end):
    center_val = (high_end + low_end) / 2.0
    half_width = (high_end - low_end) / 2.0
    sigma_val = center_val / half_width
    factor_prev = 1.0 / sigma_val
    coeffs_list = [(0.0, 1.0 / center_val)]
    for number in range(1, count_steps):
        factor_next = 1.0 / (2.0 * sigma_val - factor_prev)
        coeffs_list.append((factor_next * factor_prev, 2.0 * factor_next / half_width))
        factor_prev = factor_next
    return coeffs_list


def halve_dims(array, dims):
    for axis_num in dims:
        array = 0.5 * (
            lax.slice_in_dim(array, 0, None, 2, axis_num)
            + lax.slice_in_dim(array, 1, None, 2, axis_num)
        )
    return array


def stencil(field_ext, diff_ext, mass_core):
    field = field_ext[1:-1, 1:-1]
    diff_core = diff_ext[1:-1, 1:-1]
    low_x = 0.5 * (diff_core + diff_ext[:-2, 1:-1])
    high_x = 0.5 * (diff_core + diff_ext[2:, 1:-1])
    low_y = 0.5 * (diff_core + diff_ext[1:-1, :-2])
    high_y = 0.5 * (diff_core + diff_ext[1:-1, 2:])
    diff_zpad = jnp.pad(diff_core, ((0, 0), (0, 0), (1, 1)))
    field_zpad = jnp.pad(field, ((0, 0), (0, 0), (1, 1)))
    low_z = 0.5 * (diff_core + diff_zpad[:, :, :-2])
    high_z = 0.5 * (diff_core + diff_zpad[:, :, 2:])
    diagonal = mass_core + low_x + high_x + low_y + high_y + low_z + high_z
    neighbours = (
        low_x * field_ext[:-2, 1:-1]
        + high_x * field_ext[2:, 1:-1]
        + low_y * field_ext[1:-1, :-2]
        + high_y * field_ext[1:-1, 2:]
        + low_z * field_zpad[:, :, :-2]
        + high_z * field_zpad[:, :, 2:]
    )
    return (diagonal * field - neighbours, diagonal)


def body(source, guess, mass_coef, diffusion):
    fine_steps = cheb_coeffs(2, FINE_LOW, FINE_HIGH)

    def faces_of(field):
        return with_halo(field, (("box", 0), ("sub", 1)), 1)

    start_stack = jnp.stack([guess, diffusion])
    loop_width = 1
    loop_fields = with_halo(start_stack, (("box", 1), ("sub", 2)), loop_width)
    keep_one, gain_one = fine_steps[1]
    gain_zero = fine_steps[0][1]
    diff_loop = loop_fields[1]
    applied, diag_core = stencil(loop_fields[0], diff_loop, mass_coef)
    step_dir = gain_zero * (source - applied) / diag_core
    smoothed = guess + step_dir
    applied, unused = stencil(faces_of(smoothed), diff_loop, mass_coef)
    step_dir = keep_one * step_dir + gain_one * (source - applied) / diag_core
    smoothed = smoothed + step_dir
    applied, unused = stencil(faces_of(smoothed), diff_loop, mass_coef)
    residual = source - applied
    face_x = 0.5 * (diff_loop[:-1, 1:-1] + diff_loop[1:, 1:-1])
    face_y = 0.5 * (diff_loop[1:-1, :-1] + diff_loop[1:-1, 1:])
    diff_zpad = jnp.pad(diff_loop[1:-1, 1:-1], ((0, 0), (0, 0), (1, 1)))
    face_z = 0.5 * (diff_zpad[:, :, :-1] + diff_zpad[:, :, 1:])
    coarse_rhs = halve_dims(residual, (0, 1, 2))
    coarse_mass = halve_dims(mass_coef, (0, 1, 2))
    low_x = halve_dims(face_x[:-1:2], (1, 2))
    high_x = halve_dims(face_x[2::2], (1, 2))
    low_y = halve_dims(face_y[:, :-1:2], (0, 2))
    high_y = halve_dims(face_y[:, 2::2], (0, 2))
    low_z = halve_dims(face_z[:, :, :-1:2], (0, 1))
    high_z = halve_dims(face_z[:, :, 2::2], (0, 1))
    coarse_diag = coarse_mass + 0.25 * (low_x + high_x + low_y + high_y + low_z + high_z)
    coarse_steps = cheb_coeffs(CHEB_C, COARSE_LOW, COARSE_HIGH)
    step_dir = coarse_steps[0][1] * coarse_rhs / coarse_diag
    correction = step_dir
    for keep_part, gain_part in coarse_steps[1:]:
        extended = with_halo(correction, (("box", 0), ("sub", 1)), 1)
        corr_zpad = jnp.pad(correction, ((0, 0), (0, 0), (1, 1)))
        neighbours = (
            low_x * extended[:-2, 1:-1]
            + high_x * extended[2:, 1:-1]
            + low_y * extended[1:-1, :-2]
            + high_y * extended[1:-1, 2:]
            + low_z * corr_zpad[:, :, :-2]
            + high_z * corr_zpad[:, :, 2:]
        )
        applied = coarse_diag * correction - 0.25 * neighbours
        step_dir = keep_part * step_dir + gain_part * (coarse_rhs - applied) / coarse_diag
        correction = correction + step_dir
    prolonged = jnp.repeat(jnp.repeat(jnp.repeat(correction, 2, 0), 2, 1), 2, 2)
    field = smoothed + prolonged
    step_dir = jnp.zeros_like(field)
    for keep_part, gain_part in fine_steps:
        applied, unused = stencil(faces_of(field), diff_loop, mass_coef)
        step_dir = keep_part * step_dir + gain_part * (source - applied) / diag_core
        field = field + step_dir
    return field


def solution(mesh):
    return jax.shard_map(
        body,
        mesh=mesh,
        in_specs=(
            P("box", "sub", None),
            P("box", "sub", None),
            P("box", "sub", None),
            P("box", "sub", None),
        ),
        out_specs=P("box", "sub", None),
        check_vma=False,
    )
```

profile of v0, /device:TPU:495, one launch (start us, length us, event | category | flops | bytes accessed | tf_op | source)
XLA Modules:
  0.0 230.2 jit_solution(2114115142097215540)
XLA Ops:
  0.9 5.3 %collective-permute-start = (f32[2,1,32,256]{3,2,1,0:T(8,128)S(1)}, f32[2,1,32,256]{3,2,1,0:T(8,128)S(1)}, u32[]{:S(2)}, u32[]{:S(2)}) collective-permute-start(f32[2,1,32,256]{3,2,1,0:T(8,128)S(1)} %get-tuple-element.40), channel_id=1, source_target_pairs={{0,16},{16,32},{32,48},{48,64},{64,80},{80,96},{96,112},{112,128},... | collective-permute-start | bytes 196616 | tf_op jit(solution)/shard_map/ppermute | solution.py:20
  8.4 4.8 %collective-permute-done.1 = f32[2,1,32,256]{3,2,1,0:T(8,128)S(1)} collective-permute-done((f32[2,1,32,256]{3,2,1,0:T(8,128)S(1)}, f32[2,1,32,256]{3,2,1,0:T(8,128)S(1)}, u32[]{:S(2)}, u32[]{:S(2)}) %collective-permute-start.1) | collective-permute-done | bytes 65568 | tf_op jit(solution)/shard_map/ppermute | solution.py:23
  36.1 3.4 %collective-permute-start.7 = (f32[6,1,256]{2,1,0:T(1,128)S(1)}, f32[6,1,256]{2,1,0:T(1,128)S(1)}, u32[]{:S(2)}, u32[]{:S(2)}) collective-permute-start(f32[6,1,256]{2,1,0:T(1,128)S(1)} %get-tuple-element.49), channel_id=1, source_target_pairs={{1,0},{2,1},{3,2},{4,3},{5,4},{6,5},{7,6},{8,7},{9,8},{10,9},{11,1... | collective-permute-start | bytes 18440 | tf_op jit(solution)/shard_map/ppermute | solution.py:23
  42.8 6.0 %collective-permute-start.8 = (f32[1,32,256]{2,1,0:T(8,128)S(1)}, f32[1,32,256]{2,1,0:T(8,128)S(1)}, u32[]{:S(2)}, u32[]{:S(2)}) collective-permute-start(f32[1,32,256]{2,1,0:T(8,128)S(1)} %get-tuple-element.56), channel_id=1, source_target_pairs={{0,16},{16,32},{32,48},{48,64},{64,80},{80,96},{96,112},{112,128},... | collective-permute-start | bytes 98312 | tf_op jit(solution)/shard_map/ppermute | solution.py:20
  50.8 4.4 %collective-permute-done.9 = f32[1,32,256]{2,1,0:T(8,128)S(1)} collective-permute-done((f32[1,32,256]{2,1,0:T(8,128)S(1)}, f32[1,32,256]{2,1,0:T(8,128)S(1)}, u32[]{:S(2)}, u32[]{:S(2)}) %collective-permute-start.9) | collective-permute-done | bytes 32800 | tf_op jit(solution)/shard_map/ppermute | solution.py:23
  57.2 3.4 %collective-permute-start.11 = (f32[6,1,256]{2,1,0:T(1,128)S(1)}, f32[6,1,256]{2,1,0:T(1,128)S(1)}, u32[]{:S(2)}, u32[]{:S(2)}) collective-permute-start(f32[6,1,256]{2,1,0:T(1,128)S(1)} %get-tuple-element.47), channel_id=1, source_target_pairs={{1,0},{2,1},{3,2},{4,3},{5,4},{6,5},{7,6},{8,7},{9,8},{10,9},{11,1... | collective-permute-start | bytes 18440 | tf_op jit(solution)/shard_map/ppermute | solution.py:23
  71.4 4.2 %collective-permute-done.13 = f32[1,16,128]{2,1,0:T(8,128)S(1)} collective-permute-done((f32[1,16,128]{2,1,0:T(8,128)S(1)}, f32[1,16,128]{2,1,0:T(8,128)S(1)}, u32[]{:S(2)}, u32[]{:S(2)}) %collective-permute-start.13) | collective-permute-done | bytes 8224 | tf_op jit(solution)/shard_map/ppermute | solution.py:23
  75.7 3.7 %collective-permute-start.14 = (f32[4,1,128]{2,1,0:T(1,128)S(1)}, f32[4,1,128]{2,1,0:T(1,128)S(1)}, u32[]{:S(2)}, u32[]{:S(2)}) collective-permute-start(f32[4,1,128]{2,1,0:T(1,128)S(1)} %get-tuple-element.72), channel_id=1, source_target_pairs={{0,1},{1,2},{2,3},{3,4},{4,5},{5,6},{6,7},{7,8},{8,9},{9,10},{10,1... | collective-permute-start | bytes 6152 | tf_op jit(solution)/shard_map/ppermute | solution.py:20
  81.4 4.5 %collective-permute-done.15 = f32[4,1,128]{2,1,0:T(1,128)S(1)} collective-permute-done((f32[4,1,128]{2,1,0:T(1,128)S(1)}, f32[4,1,128]{2,1,0:T(1,128)S(1)}, u32[]{:S(2)}, u32[]{:S(2)}) %collective-permute-start.15) | collective-permute-done | bytes 2080 | tf_op jit(solution)/shard_map/ppermute | solution.py:23
  86.0 3.4 %collective-permute-start.16 = (f32[1,16,128]{2,1,0:T(8,128)S(1)}, f32[1,16,128]{2,1,0:T(8,128)S(1)}, u32[]{:S(2)}, u32[]{:S(2)}) collective-permute-start(f32[1,16,128]{2,1,0:T(8,128)S(1)} %get-tuple-element.84), channel_id=1, source_target_pairs={{0,16},{16,32},{32,48},{48,64},{64,80},{80,96},{96,112},{112,128},... | collective-permute-start | bytes 24584 | tf_op jit(solution)/shard_map/ppermute | solution.py:20
  91.3 4.2 %collective-permute-done.17 = f32[1,16,128]{2,1,0:T(8,128)S(1)} collective-permute-done((f32[1,16,128]{2,1,0:T(8,128)S(1)}, f32[1,16,128]{2,1,0:T(8,128)S(1)}, u32[]{:S(2)}, u32[]{:S(2)}) %collective-permute-start.17) | collective-permute-done | bytes 8224 | tf_op jit(solution)/shard_map/ppermute | solution.py:23
  97.5 3.4 %collective-permute-start.19 = (f32[4,1,128]{2,1,0:T(1,128)S(1)}, f32[4,1,128]{2,1,0:T(1,128)S(1)}, u32[]{:S(2)}, u32[]{:S(2)}) collective-permute-start(f32[4,1,128]{2,1,0:T(1,128)S(1)} %get-tuple-element.71), channel_id=1, source_target_pairs={{1,0},{2,1},{3,2},{4,3},{5,4},{6,5},{7,6},{8,7},{9,8},{10,9},{11,1... | collective-permute-start | bytes 6152 | tf_op jit(solution)/shard_map/ppermute | solution.py:23
  109.0 4.2 %collective-permute-done.21 = f32[1,16,128]{2,1,0:T(8,128)S(1)} collective-permute-done((f32[1,16,128]{2,1,0:T(8,128)S(1)}, f32[1,16,128]{2,1,0:T(8,128)S(1)}, u32[]{:S(2)}, u32[]{:S(2)}) %collective-permute-start.21) | collective-permute-done | bytes 8224 | tf_op jit(solution)/shard_map/ppermute | solution.py:23
  115.2 3.4 %collective-permute-start.23 = (f32[4,1,128]{2,1,0:T(1,128)S(1)}, f32[4,1,128]{2,1,0:T(1,128)S(1)}, u32[]{:S(2)}, u32[]{:S(2)}) collective-permute-start(f32[4,1,128]{2,1,0:T(1,128)S(1)} %get-tuple-element.69), channel_id=1, source_target_pairs={{1,0},{2,1},{3,2},{4,3},{5,4},{6,5},{7,6},{8,7},{9,8},{10,9},{11,1... | collective-permute-start | bytes 6152 | tf_op jit(solution)/shard_map/ppermute | solution.py:23
  126.8 4.2 %collective-permute-done.25 = f32[1,16,128]{2,1,0:T(8,128)S(1)} collective-permute-done((f32[1,16,128]{2,1,0:T(8,128)S(1)}, f32[1,16,128]{2,1,0:T(8,128)S(1)}, u32[]{:S(2)}, u32[]{:S(2)}) %collective-permute-start.25) | collective-permute-done | bytes 8224 | tf_op jit(solution)/shard_map/ppermute | solution.py:23
  133.0 3.4 %collective-permute-start.27 = (f32[4,1,128]{2,1,0:T(1,128)S(1)}, f32[4,1,128]{2,1,0:T(1,128)S(1)}, u32[]{:S(2)}, u32[]{:S(2)}) collective-permute-start(f32[4,1,128]{2,1,0:T(1,128)S(1)} %get-tuple-element.67), channel_id=1, source_target_pairs={{1,0},{2,1},{3,2},{4,3},{5,4},{6,5},{7,6},{8,7},{9,8},{10,9},{11,1... | collective-permute-start | bytes 6152 | tf_op jit(solution)/shard_map/ppermute | solution.py:23
  144.5 4.2 %collective-permute-done.29 = f32[1,16,128]{2,1,0:T(8,128)S(1)} collective-permute-done((f32[1,16,128]{2,1,0:T(8,128)S(1)}, f32[1,16,128]{2,1,0:T(8,128)S(1)}, u32[]{:S(2)}, u32[]{:S(2)}) %collective-permute-start.29) | collective-permute-done | bytes 8224 | tf_op jit(solution)/shard_map/ppermute | solution.py:23
  150.7 3.4 %collective-permute-start.31 = (f32[4,1,128]{2,1,0:T(1,128)S(1)}, f32[4,1,128]{2,1,0:T(1,128)S(1)}, u32[]{:S(2)}, u32[]{:S(2)}) collective-permute-start(f32[4,1,128]{2,1,0:T(1,128)S(1)} %get-tuple-element.65), channel_id=1, source_target_pairs={{1,0},{2,1},{3,2},{4,3},{5,4},{6,5},{7,6},{8,7},{9,8},{10,9},{11,1... | collective-permute-start | bytes 6152 | tf_op jit(solution)/shard_map/ppermute | solution.py:23
  162.3 4.2 %collective-permute-done.33 = f32[1,16,128]{2,1,0:T(8,128)S(1)} collective-permute-done((f32[1,16,128]{2,1,0:T(8,128)S(1)}, f32[1,16,128]{2,1,0:T(8,128)S(1)}, u32[]{:S(2)}, u32[]{:S(2)}) %collective-permute-start.33) | collective-permute-done | bytes 8224 | tf_op jit(solution)/shard_map/ppermute | solution.py:23
  180.0 4.2 %collective-permute-done.37 = f32[1,16,128]{2,1,0:T(8,128)S(1)} collective-permute-done((f32[1,16,128]{2,1,0:T(8,128)S(1)}, f32[1,16,128]{2,1,0:T(8,128)S(1)}, u32[]{:S(2)}, u32[]{:S(2)}) %collective-permute-start.37) | collective-permute-done | bytes 8224 | tf_op jit(solution)/shard_map/ppermute | solution.py:23
  186.2 3.4 %collective-permute-start.39 = (f32[4,1,128]{2,1,0:T(1,128)S(1)}, f32[4,1,128]{2,1,0:T(1,128)S(1)}, u32[]{:S(2)}, u32[]{:S(2)}) collective-permute-start(f32[4,1,128]{2,1,0:T(1,128)S(1)} %get-tuple-element.61), channel_id=1, source_target_pairs={{1,0},{2,1},{3,2},{4,3},{5,4},{6,5},{7,6},{8,7},{9,8},{10,9},{11,1... | collective-permute-start | bytes 6152 | tf_op jit(solution)/shard_map/ppermute | solution.py:23
  198.4 4.5 %collective-permute-done.41 = f32[1,32,256]{2,1,0:T(8,128)S(1)} collective-permute-done((f32[1,32,256]{2,1,0:T(8,128)S(1)}, f32[1,32,256]{2,1,0:T(8,128)S(1)}, u32[]{:S(2)}, u32[]{:S(2)}) %collective-permute-start.41) | collective-permute-done | bytes 32800 | tf_op jit(solution)/shard_map/ppermute | solution.py:23
  216.5 4.5 %collective-permute-done.45 = f32[1,32,256]{2,1,0:T(8,128)S(1)} collective-permute-done((f32[1,32,256]{2,1,0:T(8,128)S(1)}, f32[1,32,256]{2,1,0:T(8,128)S(1)}, u32[]{:S(2)}, u32[]{:S(2)}) %collective-permute-start.45) | collective-permute-done | bytes 32800 | tf_op jit(solution)/shard_map/ppermute | solution.py:23
  222.9 3.4 %collective-permute-start.47 = (f32[6,1,256]{2,1,0:T(1,128)S(1)}, f32[6,1,256]{2,1,0:T(1,128)S(1)}, u32[]{:S(2)}, u32[]{:S(2)}) collective-permute-start(f32[6,1,256]{2,1,0:T(1,128)S(1)} %get-tuple-element.43), channel_id=1, source_target_pairs={{1,0},{2,1},{3,2},{4,3},{5,4},{6,5},{7,6},{8,7},{9,8},{10,9},{11,1... | collective-permute-start | bytes 18440 | tf_op jit(solution)/shard_map/ppermute | solution.py:23
  (173 shorter events, 131.4 us)
Async XLA Ops:
  0.9 7.5 %collective-permute-start = (f32[2,1,32,256]{3,2,1,0:T(8,128)S(1)}, f32[2,1,32,256]{3,2,1,0:T(8,128)S(1)}, u32[]{:S(2)}, u32[]{:S(2)}) collective-permute-start(f32[2,1,32,256]{3,2,1,0:T(8,128)S(1)} %get-tuple-element.40), channel_id=1, source_target_pairs={{0,16},{16,32},{32,48},{48,64},{64,80},{80,96},{96,112},{112,128},... | collective-permute-start | bytes 196616 | tf_op jit(solution)/shard_map/ppermute | solution.py:20
  6.2 6.9 %collective-permute-start.1 = (f32[2,1,32,256]{3,2,1,0:T(8,128)S(1)}, f32[2,1,32,256]{3,2,1,0:T(8,128)S(1)}, u32[]{:S(2)}, u32[]{:S(2)}) collective-permute-start(f32[2,1,32,256]{3,2,1,0:T(8,128)S(1)} %get-tuple-element.41), channel_id=1, source_target_pairs={{16,0},{32,16},{48,32},{64,48},{80,64},{96,80},{112,96},{128,112},... | collective-permute-start | bytes 196616 | tf_op jit(solution)/shard_map/ppermute | solution.py:23
  13.2 6.5 %collective-permute-start.2 = (f32[2,6,1,256]{3,0,2,1:T(2,128)S(1)}, f32[2,6,1,256]{3,0,2,1:T(2,128)S(1)}, u32[]{:S(2)}, u32[]{:S(2)}) collective-permute-start(f32[2,6,1,256]{3,0,2,1:T(2,128)S(1)} %copy.282), channel_id=1, source_target_pairs={{0,1},{1,2},{2,3},{3,4},{4,5},{5,6},{6,7},{7,8},{8,9},{9,10},{10,1... | collective-permute-start | bytes 36872 | tf_op jit(solution)/shard_map/ppermute | solution.py:20
  16.3 6.5 %collective-permute-start.3 = (f32[2,6,1,256]{3,0,2,1:T(2,128)S(1)}, f32[2,6,1,256]{3,0,2,1:T(2,128)S(1)}, u32[]{:S(2)}, u32[]{:S(2)}) collective-permute-start(f32[2,6,1,256]{3,0,2,1:T(2,128)S(1)} %copy.283), channel_id=1, source_target_pairs={{1,0},{2,1},{3,2},{4,3},{5,4},{6,5},{7,6},{8,7},{9,8},{10,9},{11,1... | collective-permute-start | bytes 36872 | tf_op jit(solution)/shard_map/ppermute | solution.py:23
  24.4 9.7 %collective-permute-start.4 = (f32[1,32,256]{2,1,0:T(8,128)S(1)}, f32[1,32,256]{2,1,0:T(8,128)S(1)}, u32[]{:S(2)}, u32[]{:S(2)}) collective-permute-start(f32[1,32,256]{2,1,0:T(8,128)S(1)} %get-tuple-element.58), channel_id=1, source_target_pairs={{0,16},{16,32},{32,48},{48,64},{64,80},{80,96},{96,112},{112,128},... | collective-permute-start | bytes 98312 | tf_op jit(solution)/shard_map/ppermute | solution.py:20
  27.7 6.4 %collective-permute-start.5 = (f32[1,32,256]{2,1,0:T(8,128)S(1)}, f32[1,32,256]{2,1,0:T(8,128)S(1)}, u32[]{:S(2)}, u32[]{:S(2)}) collective-permute-start(f32[1,32,256]{2,1,0:T(8,128)S(1)} %get-tuple-element.59), channel_id=1, source_target_pairs={{16,0},{32,16},{48,32},{64,48},{80,64},{96,80},{112,96},{128,112},... | collective-permute-start | bytes 98312 | tf_op jit(solution)/shard_map/ppermute | solution.py:23
  36.1 6.5 %collective-permute-start.7 = (f32[6,1,256]{2,1,0:T(1,128)S(1)}, f32[6,1,256]{2,1,0:T(1,128)S(1)}, u32[]{:S(2)}, u32[]{:S(2)}) collective-permute-start(f32[6,1,256]{2,1,0:T(1,128)S(1)} %get-tuple-element.49), channel_id=1, source_target_pairs={{1,0},{2,1},{3,2},{4,3},{5,4},{6,5},{7,6},{8,7},{9,8},{10,9},{11,1... | collective-permute-start | bytes 18440 | tf_op jit(solution)/shard_map/ppermute | solution.py:23
  42.8 8.0 %collective-permute-start.8 = (f32[1,32,256]{2,1,0:T(8,128)S(1)}, f32[1,32,256]{2,1,0:T(8,128)S(1)}, u32[]{:S(2)}, u32[]{:S(2)}) collective-permute-start(f32[1,32,256]{2,1,0:T(8,128)S(1)} %get-tuple-element.56), channel_id=1, source_target_pairs={{0,16},{16,32},{32,48},{48,64},{64,80},{80,96},{96,112},{112,128},... | collective-permute-start | bytes 98312 | tf_op jit(solution)/shard_map/ppermute | solution.py:20
  48.8 6.4 %collective-permute-start.9 = (f32[1,32,256]{2,1,0:T(8,128)S(1)}, f32[1,32,256]{2,1,0:T(8,128)S(1)}, u32[]{:S(2)}, u32[]{:S(2)}) collective-permute-start(f32[1,32,256]{2,1,0:T(8,128)S(1)} %get-tuple-element.57), channel_id=1, source_target_pairs={{16,0},{32,16},{48,32},{64,48},{80,64},{96,80},{112,96},{128,112},... | collective-permute-start | bytes 98312 | tf_op jit(solution)/shard_map/ppermute | solution.py:23
  55.2 10.2 %collective-permute-start.10 = (f32[6,1,256]{2,1,0:T(1,128)S(1)}, f32[6,1,256]{2,1,0:T(1,128)S(1)}, u32[]{:S(2)}, u32[]{:S(2)}) collective-permute-start(f32[6,1,256]{2,1,0:T(1,128)S(1)} %get-tuple-element.46), channel_id=1, source_target_pairs={{0,1},{1,2},{2,3},{3,4},{4,5},{5,6},{6,7},{7,8},{8,9},{9,10},{10,1... | collective-permute-start | bytes 18440 | tf_op jit(solution)/shard_map/ppermute | solution.py:20
  57.2 8.3 %collective-permute-start.11 = (f32[6,1,256]{2,1,0:T(1,128)S(1)}, f32[6,1,256]{2,1,0:T(1,128)S(1)}, u32[]{:S(2)}, u32[]{:S(2)}) collective-permute-start(f32[6,1,256]{2,1,0:T(1,128)S(1)} %get-tuple-element.47), channel_id=1, source_target_pairs={{1,0},{2,1},{3,2},{4,3},{5,4},{6,5},{7,6},{8,7},{9,8},{10,9},{11,1... | collective-permute-start | bytes 18440 | tf_op jit(solution)/shard_map/ppermute | solution.py:23
  79.4 6.4 %collective-permute-start.15 = (f32[4,1,128]{2,1,0:T(1,128)S(1)}, f32[4,1,128]{2,1,0:T(1,128)S(1)}, u32[]{:S(2)}, u32[]{:S(2)}) collective-permute-start(f32[4,1,128]{2,1,0:T(1,128)S(1)} %get-tuple-element.73), channel_id=1, source_target_pairs={{1,0},{2,1},{3,2},{4,3},{5,4},{6,5},{7,6},{8,7},{9,8},{10,9},{11,1... | collective-permute-start | bytes 6152 | tf_op jit(solution)/shard_map/ppermute | solution.py:23
  97.5 6.4 %collective-permute-start.19 = (f32[4,1,128]{2,1,0:T(1,128)S(1)}, f32[4,1,128]{2,1,0:T(1,128)S(1)}, u32[]{:S(2)}, u32[]{:S(2)}) collective-permute-start(f32[4,1,128]{2,1,0:T(1,128)S(1)} %get-tuple-element.71), channel_id=1, source_target_pairs={{1,0},{2,1},{3,2},{4,3},{5,4},{6,5},{7,6},{8,7},{9,8},{10,9},{11,1... | collective-permute-start | bytes 6152 | tf_op jit(solution)/shard_map/ppermute | solution.py:23
  107.1 6.2 %collective-permute-start.21 = (f32[1,16,128]{2,1,0:T(8,128)S(1)}, f32[1,16,128]{2,1,0:T(8,128)S(1)}, u32[]{:S(2)}, u32[]{:S(2)}) collective-permute-start(f32[1,16,128]{2,1,0:T(8,128)S(1)} %get-tuple-element.83), channel_id=1, source_target_pairs={{16,0},{32,16},{48,32},{64,48},{80,64},{96,80},{112,96},{128,112},... | collective-permute-start | bytes 24584 | tf_op jit(solution)/shard_map/ppermute | solution.py:23
  115.2 6.4 %collective-permute-start.23 = (f32[4,1,128]{2,1,0:T(1,128)S(1)}, f32[4,1,128]{2,1,0:T(1,128)S(1)}, u32[]{:S(2)}, u32[]{:S(2)}) collective-permute-start(f32[4,1,128]{2,1,0:T(1,128)S(1)} %get-tuple-element.69), channel_id=1, source_target_pairs={{1,0},{2,1},{3,2},{4,3},{5,4},{6,5},{7,6},{8,7},{9,8},{10,9},{11,1... | collective-permute-start | bytes 6152 | tf_op jit(solution)/shard_map/ppermute | solution.py:23
  133.0 6.4 %collective-permute-start.27 = (f32[4,1,128]{2,1,0:T(1,128)S(1)}, f32[4,1,128]{2,1,0:T(1,128)S(1)}, u32[]{:S(2)}, u32[]{:S(2)}) collective-permute-start(f32[4,1,128]{2,1,0:T(1,128)S(1)} %get-tuple-element.67), channel_id=1, source_target_pairs={{1,0},{2,1},{3,2},{4,3},{5,4},{6,5},{7,6},{8,7},{9,8},{10,9},{11,1... | collective-permute-start | bytes 6152 | tf_op jit(solution)/shard_map/ppermute | solution.py:23
  150.7 6.4 %collective-permute-start.31 = (f32[4,1,128]{2,1,0:T(1,128)S(1)}, f32[4,1,128]{2,1,0:T(1,128)S(1)}, u32[]{:S(2)}, u32[]{:S(2)}) collective-permute-start(f32[4,1,128]{2,1,0:T(1,128)S(1)} %get-tuple-element.65), channel_id=1, source_target_pairs={{1,0},{2,1},{3,2},{4,3},{5,4},{6,5},{7,6},{8,7},{9,8},{10,9},{11,1... | collective-permute-start | bytes 6152 | tf_op jit(solution)/shard_map/ppermute | solution.py:23
  160.3 6.2 %collective-permute-start.33 = (f32[1,16,128]{2,1,0:T(8,128)S(1)}, f32[1,16,128]{2,1,0:T(8,128)S(1)}, u32[]{:S(2)}, u32[]{:S(2)}) collective-permute-start(f32[1,16,128]{2,1,0:T(8,128)S(1)} %get-tuple-element.77), channel_id=1, source_target_pairs={{16,0},{32,16},{48,32},{64,48},{80,64},{96,80},{112,96},{128,112},... | collective-permute-start | bytes 24584 | tf_op jit(solution)/shard_map/ppermute | solution.py:23
  168.5 6.4 %collective-permute-start.35 = (f32[4,1,128]{2,1,0:T(1,128)S(1)}, f32[4,1,128]{2,1,0:T(1,128)S(1)}, u32[]{:S(2)}, u32[]{:S(2)}) collective-permute-start(f32[4,1,128]{2,1,0:T(1,128)S(1)} %get-tuple-element.63), channel_id=1, source_target_pairs={{1,0},{2,1},{3,2},{4,3},{5,4},{6,5},{7,6},{8,7},{9,8},{10,9},{11,1... | collective-permute-start | bytes 6152 | tf_op jit(solution)/shard_map/ppermute | solution.py:23
  186.2 6.4 %collective-permute-start.39 = (f32[4,1,128]{2,1,0:T(1,128)S(1)}, f32[4,1,128]{2,1,0:T(1,128)S(1)}, u32[]{:S(2)}, u32[]{:S(2)}) collective-permute-start(f32[4,1,128]{2,1,0:T(1,128)S(1)} %get-tuple-element.61), channel_id=1, source_target_pairs={{1,0},{2,1},{3,2},{4,3},{5,4},{6,5},{7,6},{8,7},{9,8},{10,9},{11,1... | collective-permute-start | bytes 6152 | tf_op jit(solution)/shard_map/ppermute | solution.py:23
  196.4 6.4 %collective-permute-start.41 = (f32[1,32,256]{2,1,0:T(8,128)S(1)}, f32[1,32,256]{2,1,0:T(8,128)S(1)}, u32[]{:S(2)}, u32[]{:S(2)}) collective-permute-start(f32[1,32,256]{2,1,0:T(8,128)S(1)} %get-tuple-element.55), channel_id=1, source_target_pairs={{16,0},{32,16},{48,32},{64,48},{80,64},{96,80},{112,96},{128,112},... | collective-permute-start | bytes 98312 | tf_op jit(solution)/shard_map/ppermute | solution.py:23
  204.8 6.5 %collective-permute-start.43 = (f32[6,1,256]{2,1,0:T(1,128)S(1)}, f32[6,1,256]{2,1,0:T(1,128)S(1)}, u32[]{:S(2)}, u32[]{:S(2)}) collective-permute-start(f32[6,1,256]{2,1,0:T(1,128)S(1)} %get-tuple-element.45), channel_id=1, source_target_pairs={{1,0},{2,1},{3,2},{4,3},{5,4},{6,5},{7,6},{8,7},{9,8},{10,9},{11,1... | collective-permute-start | bytes 18440 | tf_op jit(solution)/shard_map/ppermute | solution.py:23
  214.5 6.4 %collective-permute-start.45 = (f32[1,32,256]{2,1,0:T(8,128)S(1)}, f32[1,32,256]{2,1,0:T(8,128)S(1)}, u32[]{:S(2)}, u32[]{:S(2)}) collective-permute-start(f32[1,32,256]{2,1,0:T(8,128)S(1)} %get-tuple-element.53), channel_id=1, source_target_pairs={{16,0},{32,16},{48,32},{64,48},{80,64},{96,80},{112,96},{128,112},... | collective-permute-start | bytes 98312 | tf_op jit(solution)/shard_map/ppermute | solution.py:23
  222.9 6.5 %collective-permute-start.47 = (f32[6,1,256]{2,1,0:T(1,128)S(1)}, f32[6,1,256]{2,1,0:T(1,128)S(1)}, u32[]{:S(2)}, u32[]{:S(2)}) collective-permute-start(f32[6,1,256]{2,1,0:T(1,128)S(1)} %get-tuple-element.43), channel_id=1, source_target_pairs={{1,0},{2,1},{3,2},{4,3},{5,4},{6,5},{7,6},{8,7},{9,8},{10,9},{11,1... | collective-permute-start | bytes 18440 | tf_op jit(solution)/shard_map/ppermute | solution.py:23
  (28 other events, 152.3 us)
where the time goes:
time: 232 us; the launch traced here: 230 us
  starting transfers between devices  129 us (56%)
  waiting for transfers between devices  83.3 us (36%)
  local copies, waits for them, and re-layouts  13.4 us (6%)
  other arithmetic  3.52 us (2%)
    ppermute x24, waiting for transfers between devices, with_halo(): lax.ppermute(lax.slice_in_dim(block, 0, width, axis=dim), axis, backward)  83.2 us
    ppermute x24, starting transfers between devices, with_halo(): lax.ppermute(lax.slice_in_dim(block, block.shape[dim] - width, None, axis...  68.1 us
    ppermute x24, starting transfers between devices, with_halo(): lax.ppermute(lax.slice_in_dim(block, 0, width, axis=dim), axis, backward)  60.9 us
  transfers between devices with their start and end apart: 48, of which 22 were waited for; matrix products, arithmetic and copies ran while one was open for 5% of the time, Pallas kernels for 0%

commit v1 on v0

v1 whole, which is shorter than its diff:
```python
import functools

import jax
import jax.numpy as jnp
from jax import lax
from jax.experimental import pallas as pl
from jax.experimental.pallas import tpu as pltpu
from jax.sharding import PartitionSpec as P

MESH = pl.DeviceIdType.MESH
CHEB_C = 8
FINE_LOW = 0.25
FINE_HIGH = 2.0
COARSE_LOW = 0.05
COARSE_HIGH = 2.0

FX0, FX1, FR0, FRN = 3, 7, 4, 32
CX0, CR0, CRN = 4, 4, 16
GUESS, DIFF, SOURCE, MASS = 0, 1, 2, 3

NEAR = [(i, j) for i in (-2, 2, -1, 1) for j in (-1, 1)] + [(-2, 0), (2, 0), (0, -1), (0, 1), (-1, 0), (1, 0)]
RING = [(i, j) for i in (-1, 1) for j in (-1, 1)] + [(0, -1), (0, 1), (-1, 0), (1, 0)]


def cheb_coeffs(count_steps, low_end, high_end):
    center_val = (high_end + low_end) / 2.0
    half_width = (high_end - low_end) / 2.0
    sigma_val = center_val / half_width
    factor_prev = 1.0 / sigma_val
    coeffs_list = [(0.0, 1.0 / center_val)]
    for number in range(1, count_steps):
        factor_next = 1.0 / (2.0 * sigma_val - factor_prev)
        coeffs_list.append((factor_next * factor_prev, 2.0 * factor_next / half_width))
        factor_prev = factor_next
    return coeffs_list


def coarse_rows(os):
    if os == 1:
        return pl.ds(CR0 + CRN - 4, 4), pl.ds(0, 4)
    if os == -1:
        return pl.ds(CR0, 4), pl.ds(CR0 + CRN, 4)
    return pl.ds(CR0, CRN), pl.ds(CR0, CRN)


def fine_cut(o, start, size, width):
    if o == 1:
        return pl.ds(start + size - width, width), pl.ds(start - width, width)
    if o == -1:
        return pl.ds(start, width), pl.ds(start + size, width)
    return pl.ds(start, size), pl.ds(start, size)


def rim_messages():
    found = []
    for i in (-1, 1):
        found.append(((i, 0), pl.ds(0, 2), 3, FRN))
    for i in (-1, 1):
        for j in (-1, 1):
            found.append(((i, j), pl.ds(0, 4), 2, 2))
    for j in (-1, 1):
        found.append(((0, j), pl.ds(0, 4), 4, 3))
    for i in (-1, 1):
        found.append(((i, 0), pl.ds(2, 2), 2, FRN))
    return found


def dot(a, b):
    return jnp.dot(a, b, precision=lax.Precision.HIGHEST, preferred_element_type=jnp.float32)


def kernel(source, guess, mass, diff, out, F, FX, FY, FZ, DIAG, INV, W1, W2, DIR, RES, L2, C, G, A, B, XA, XB, CD,
           load_sem, r_send, r_recv, c_send, c_recv, e_send, e_recv, b_send, b_recv, l_send, l_recv):
    f32 = jnp.float32
    nbox, nsub = lax.axis_size("box"), lax.axis_size("sub")
    b, s = lax.axis_index("box"), lax.axis_index("sub")

    def device(o):
        return (lax.rem(b + o[0] + nbox, nbox), lax.rem(s + o[1] + nsub, nsub))

    loads = []
    for k, ref in enumerate((guess, diff, source, mass)):
        for h in range(2):
            loads.append(pltpu.make_async_copy(
                ref.at[:, :, pl.ds(128 * h, 128)], F.at[k, pl.ds(FX0, 4), h, pl.ds(FR0, FRN)], load_sem.at[k, h]))
            loads[-1].start()
    barrier = pltpu.get_barrier_semaphore()
    for o in NEAR:
        pl.semaphore_signal(barrier, inc=1, device_id=device(o), device_id_type=MESH)
    for load in loads:
        load.wait()
    pl.semaphore_wait(barrier, len(NEAR))

    first = []
    for k, (o, arrays, xw, rw) in enumerate(rim_messages()):
        xs, xd = fine_cut(o[0], FX0, 4, xw)
        rs, rd = fine_cut(o[1], FR0, FRN, rw)
        first.append(pltpu.make_async_remote_copy(
            src_ref=F.at[arrays, xs, :, rs], dst_ref=F.at[arrays, xd, :, rd],
            send_sem=r_send.at[k], recv_sem=r_recv.at[k], device_id=device(o), device_id_type=MESH))
        first[-1].start()

    lane = lax.broadcasted_iota(jnp.int32, (256, 128), 0)
    cell = lax.broadcasted_iota(jnp.int32, (256, 128), 1)
    z_mean = jnp.where(lax.shift_right_logical(lane, 1) == cell, f32(0.5), f32(0.0))
    z_low = jnp.where(lax.shift_right_logical(lane + 1, 1) == cell, f32(0.5), f32(0.0))
    z_high = jnp.where(lax.shift_right_logical(lane + 1, 1) == cell + 1, f32(0.5), f32(0.0))
    row = lax.broadcasted_iota(jnp.int32, (2, 40, 128), 1)
    row_in = jnp.logical_and(jnp.logical_or(row >= FR0, s > 0), jnp.logical_or(row < FR0 + FRN, s < nsub - 1))
    row_mask = jnp.where(row_in, f32(1.0), f32(0.0))
    lane_f = lax.broadcasted_iota(jnp.int32, (2, 40, 128), 2)
    half = lax.broadcasted_iota(jnp.int32, (2, 40, 128), 0)
    z_first = jnp.logical_and(lane_f == 0, half == 0)
    z_last = jnp.logical_and(lane_f == 127, half == 1)

    def shift(v, edge, by):
        r = pltpu.roll(v, by, 2)
        return jnp.where(edge, jnp.stack([r[1], r[0]]), r)

    def from_below(v):
        return shift(v, lane_f == 0, 1)

    def from_above(v):
        return shift(v, lane_f == 127, 127)


    def slab_in(x):
        inside = jnp.logical_and(jnp.logical_or(x >= FX0, b > 0), jnp.logical_or(x < FX1, b < nbox - 1))
        return jnp.where(inside, f32(1.0), f32(0.0))

    for message in first:
        message.wait_recv()

    @pl.when(b == 0)
    def _():
        F[0:2, 0:FX0] = jnp.zeros((2, FX0, 2, 40, 128), f32)

    @pl.when(b == nbox - 1)
    def _():
        F[0:2, FX1:10] = jnp.zeros((2, 10 - FX1, 2, 40, 128), f32)

    @pl.when(s == 0)
    def _():
        F[0:2, :, :, 0:FR0] = jnp.zeros((2, 10, 2, FR0, 128), f32)

    @pl.when(s == nsub - 1)
    def _():
        F[0:2, :, :, FR0 + FRN:40] = jnp.zeros((2, 10, 2, 40 - FR0 - FRN, 128), f32)

    def rows(ref, x, start):
        return ref[x, :, pl.ds(start, 16, 2), :]

    def wide(parts):
        return jnp.concatenate([jnp.concatenate([v[0], v[1]], 1) for v in parts], 0)


    D, M = F.at[DIFF], F.at[MASS]
    pair = {x: rows(D, x, FR0) + rows(D, x, FR0 + 1) for x in range(FX0 - 1, FX1 + 1)}
    low_y = {x: rows(D, x, FR0 - 1) + rows(D, x, FR0) for x in range(FX0, FX1)}
    high_y = {x: rows(D, x, FR0 + 1) + rows(D, x, FR0 + 2) for x in range(FX0, FX1)}
    in_mean, in_z = [], []
    for X in range(2):
        x = FX0 + 2 * X
        face_low, face_high = 0.25 * (pair[x - 1] + pair[x]), 0.25 * (pair[x + 1] + pair[x + 2])
        y_low, y_high = 0.25 * (low_y[x] + low_y[x + 1]), 0.25 * (high_y[x] + high_y[x + 1])
        mean_mass = 0.25 * (rows(M, x, FR0) + rows(M, x, FR0 + 1) + rows(M, x + 1, FR0) + rows(M, x + 1, FR0 + 1))
        in_mean += [face_low, y_low, mean_mass + 0.25 * (face_low + face_high + y_low + y_high)]
        in_z.append(0.25 * (pair[x] + pair[x + 1]))
    means = dot(wide(in_mean), z_mean)
    over_z = wide(in_z)
    lows_z, highs_z = dot(over_z, z_low), dot(over_z, z_high)
    own_s = []
    for X in range(2):
        fx, fy, d = (means[(3 * X + k) * 16:(3 * X + k + 1) * 16] for k in range(3))
        fz = lows_z[16 * X:16 * X + 16]
        d = d + 0.25 * (fz + highs_z[16 * X:16 * X + 16])
        sc = lax.rsqrt(d)
        sc = sc * (1.5 - 0.5 * d * sc * sc)
        own_s.append(sc)
        for k, v in enumerate((fx, fy, fz, sc)):
            C[k, CX0 + X, pl.ds(CR0, CRN), :] = v

    def coarse_messages(src, lead, sends, recvs):
        found = []
        for k, o in enumerate(NEAR):
            rs, rd = coarse_rows(o[1])
            at_src = lead + (pl.ds(CX0, 2), rs)
            at_dst = lead + (pl.ds(CX0 - 2 * o[0], 2), rd)
            found.append(pltpu.make_async_remote_copy(
                src_ref=src.at[at_src], dst_ref=src.at[at_dst],
                send_sem=sends.at[k], recv_sem=recvs.at[k], device_id=device(o), device_id_type=MESH))
            found[-1].start()
        return found

    coefs = coarse_messages(C, (pl.ds(0, 4),), c_send, c_recv)

    def face_body(x, carry):
        FX[x] = 0.5 * (F[DIFF, x - 1] + F[DIFF, x])
        return carry

    lax.fori_loop(1, 10, face_body, 0)

    def operator_body(x, carry):
        d = F[DIFF, x]
        fy = 0.5 * (d + pltpu.roll(d, 1, 1))
        fz = 0.5 * (d + jnp.where(z_first, f32(0.0), from_below(d)))
        fz_high = 0.5 * (d + jnp.where(z_last, f32(0.0), from_above(d)))
        diag = F[MASS, x] + FX[x] + FX[x + 1] + fy + pltpu.roll(fy, 39, 1) + fz + fz_high
        FY[x] = fy
        FZ[x] = jnp.where(z_first, f32(0.0), fz)
        DIAG[x] = diag
        INV[x] = (row_mask * slab_in(x)) / diag
        return carry

    lax.fori_loop(1, 9, operator_body, 0)

    def defect(u_ref, x):
        u = u_ref[x]
        fy, fz = FY[x], FZ[x]
        around = FX[x] * u_ref[x - 1] + FX[x + 1] * u_ref[x + 1]
        around = around + fy * pltpu.roll(u, 1, 1) + pltpu.roll(fy * u, 39, 1)
        around = around + fz * from_below(u) + from_above(fz * u)
        return (F[SOURCE, x] - DIAG[x] * u) + around, u

    fine = cheb_coeffs(2, FINE_LOW, FINE_HIGH)
    coarse = cheb_coeffs(CHEB_C, COARSE_LOW, COARSE_HIGH)

    def first_step(u_ref, to_ref):
        def body(x, carry):
            c, u = defect(u_ref, x)
            step_dir = (fine[0][1] * INV[x]) * c
            DIR[x] = step_dir
            to_ref[x] = u + step_dir
            return carry

        return body

    lax.fori_loop(1, 9, first_step(F.at[GUESS], W1), 0)

    def second_step(x):
        c, u = defect(W1, x)
        return u + (fine[1][0] * DIR[x] + (fine[1][1] * INV[x]) * c)

    def second_body(x, carry):
        W2[x] = second_step(x)
        return carry

    lax.fori_loop(2, 8, second_body, 0)

    def residual_body(x, carry):
        RES[x] = defect(W2, x)[0]
        return carry

    lax.fori_loop(FX0, FX1, residual_body, 0)

    means = []
    for X in range(2):
        x = FX0 + 2 * X
        means.append(0.25 * ((rows(RES, x, FR0) + rows(RES, x, FR0 + 1)) + (rows(RES, x + 1, FR0) + rows(RES, x + 1, FR0 + 1))))
    rhs = dot(wide(means), z_mean)
    for X in range(2):
        A[CX0 + X, pl.ds(CR0, CRN), :] = own_s[X] * rhs[16 * X:16 * X + 16]
    e_one = coarse_messages(A, (), e_send, e_recv)

    for x in range(FX0, FX1):
        L2[x, :, pl.ds(FR0, FRN), :] = W2[x, :, pl.ds(FR0, FRN), :]
    late = []
    for k, o in enumerate(RING):
        xs, xd = fine_cut(o[0], FX0, 4, 2)
        rs, rd = fine_cut(o[1], FR0, FRN, 2)
        late.append(pltpu.make_async_remote_copy(
            src_ref=L2.at[xs, :, rs], dst_ref=L2.at[xd, :, rd],
            send_sem=l_send.at[k], recv_sem=l_recv.at[k], device_id=device(o), device_id_type=MESH))
        late[-1].start()

    for message in coefs:
        message.wait_recv()
    crow = lax.broadcasted_iota(jnp.int32, (24, 128), 0)
    clane = lax.broadcasted_iota(jnp.int32, (24, 128), 1)
    first_row = jnp.logical_or(jnp.logical_and(s == 0, crow == CR0), jnp.logical_and(s == nsub - 1, crow == CR0 + CRN))
    for X in range(10):
        sc = C[3, X]
        if X > 0:
            edge = lax.rem(2 * b + (X - CX0) + 2 * nbox, 2 * nbox) == 0
            G[0, X] = C[0, X] * ((0.25 * sc) * C[3, X - 1]) * jnp.where(edge, f32(0.0), f32(1.0))
        G[1, X] = jnp.where(first_row, f32(0.0), C[1, X] * ((0.25 * sc) * pltpu.roll(sc, 1, 0)))
        G[2, X] = jnp.where(clane == 0, f32(0.0), C[2, X] * ((0.25 * sc) * pltpu.roll(sc, 1, 1)))

    def coarse_step(x_ref, d_ref, to_x, to_d, X, number):
        keep, gain = coarse[number]
        x = x_ref[X]
        gy, gz = G[1, X], G[2, X]
        c = (A[X] - x) + G[0, X] * x_ref[X - 1] + G[0, X + 1] * x_ref[X + 1]
        c = c + gy * pltpu.roll(x, 1, 0) + pltpu.roll(gy * x, 23, 0)
        c = c + gz * pltpu.roll(x, 1, 1) + pltpu.roll(gz * x, 127, 1)
        step_dir = keep * d_ref[X] + gain * c
        return x + step_dir, step_dir

    for message in e_one:
        message.wait_recv()
    for X in range(10):
        start = coarse[0][1] * A[X]
        XA[X] = start
        CD[X] = start
    now, later = XA, XB
    for number in range(1, 4):
        for X in range(number, 10 - number):
            later[X], CD[X] = coarse_step(now, CD, None, None, X, number)
        now, later = later, now
    for X in range(CX0, CX0 + 2):
        new_x, new_d = coarse_step(now, CD, None, None, X, 4)
        B[0, X, pl.ds(CR0, CRN), :] = new_x[CR0:CR0 + CRN]
        B[1, X, pl.ds(CR0, CRN), :] = new_d[CR0:CR0 + CRN]
    e_two = coarse_messages(B, (pl.ds(0, 2),), b_send, b_recv)
    for message in e_two:
        message.wait_recv()
    now, now_d = B.at[0], B.at[1]
    for number, later in ((5, XA), (6, XB), (7, XA)):
        for X in range(number - 4, 14 - number):
            later[X], CD[X] = coarse_step(now, now_d, None, None, X, number)
        now, now_d = later, CD

    for message in late:
        message.wait_recv()
    spread_z = jnp.where(
        lax.shift_right_logical(lax.broadcasted_iota(jnp.int32, (128, 256), 1), 1) == lax.broadcasted_iota(jnp.int32, (128, 256), 0),
        f32(1.0), f32(0.0))
    spread_y = jnp.where(
        lax.shift_right_logical(lax.broadcasted_iota(jnp.int32, (40, 24), 0) + (2 * CR0 - FR0), 1) == lax.broadcasted_iota(jnp.int32, (40, 24), 1),
        f32(1.0), f32(0.0))
    corr = jnp.concatenate([C[3, X] * now[X] for X in range(3, 7)], 0)
    corr = dot(corr, spread_z)
    for X in range(4):
        fine_corr = dot(spread_y, corr[24 * X:24 * X + 24])
        fine_corr = jnp.stack([fine_corr[:, :128], fine_corr[:, 128:]])
        for x in (2 * X + 1, 2 * X + 2):
            W2[x] = (L2[x] + fine_corr) * (row_mask * slab_in(x))

    def third_body(x, carry):
        return first_step(W2, W1)(x, carry)

    lax.fori_loop(2, 8, third_body, 0)
    for x in range(FX0, FX1):
        last = second_step(x)
        for h in range(2):
            out[x - FX0, :, 128 * h:128 * h + 128] = last[h, FR0:FR0 + FRN]

    for message in first + coefs + e_one + late + e_two:
        message.wait_send()


def body(source, guess, mass_coef, diffusion):
    vmem = pltpu.VMEM
    fine_slabs = lambda: vmem((10, 2, 40, 128), jnp.float32)
    coarse_slabs = lambda: vmem((10, 24, 128), jnp.float32)
    n_rim, n_near, n_ring = len(rim_messages()), len(NEAR), len(RING)
    dma = pltpu.SemaphoreType.DMA
    return pl.pallas_call(
        kernel,
        out_shape=jax.ShapeDtypeStruct((4, 32, 256), jnp.float32),
        in_specs=[pl.BlockSpec(memory_space=pl.ANY)] * 4,
        out_specs=pl.BlockSpec(memory_space=pltpu.VMEM),
        scratch_shapes=[
            vmem((4, 10, 2, 40, 128), jnp.float32),
            fine_slabs(), fine_slabs(), fine_slabs(), fine_slabs(), fine_slabs(),
            fine_slabs(), fine_slabs(), fine_slabs(), fine_slabs(), fine_slabs(),
            vmem((4, 10, 24, 128), jnp.float32),
            vmem((3, 10, 24, 128), jnp.float32),
            coarse_slabs(),
            vmem((2, 10, 24, 128), jnp.float32),
            coarse_slabs(), coarse_slabs(), coarse_slabs(),
            dma((4, 2)),
            dma((n_rim,)), dma((n_rim,)),
            dma((n_near,)), dma((n_near,)),
            dma((n_near,)), dma((n_near,)),
            dma((n_near,)), dma((n_near,)),
            dma((n_ring,)), dma((n_ring,)),
        ],
        compiler_params=pltpu.CompilerParams(collective_id=0, has_side_effects=True, vmem_limit_bytes=48 * 2**20),
        name="cycle",
    )(source, guess, mass_coef, diffusion)


def solution(mesh):
    spec = P("box", "sub", None)
    return jax.shard_map(body, mesh=mesh, in_specs=(spec,) * 4, out_specs=spec, check_vma=False)
```

time: 232 us -> 51.6 us (0.22)
  the two profiles are of different devices: /device:TPU:495 before, /device:TPU:1 now
where the time goes in v1:
time: 51.6 us; the launch traced here: 51.3 us
  Pallas kernels  47.1 us (91%)
  local copies, waits for them, and re-layouts  4.27 us (8%)
    pallas_call x1, Pallas kernels, body(): pl.pallas_call(kernel, out_shape=jax.ShapeDtypeStruct((4, 32, 256), jnp.f...  47.1 us
    unnamed x9, local copies, waits for them, and re-layouts  4.27 us

profile of v1, /device:TPU:1, one launch (start us, length us, event | category | flops | bytes accessed | tf_op | source)
XLA Modules:
  0.0 51.3 jit_solution(14634934030418408617)
XLA Ops:
  0.0 0.0 copy-start
  0.0 0.9 %copy-done = f32[4,32,256]{2,1,0:T(8,128)S(1)} copy-done((f32[4,32,256]{2,1,0:T(8,128)S(1)}, f32[4,32,256]{2,1,0:T(8,128)}, u32[]{:S(2)}) %copy-start) | copy-done | bytes 131096
  0.9 0.0 copy-start.1
  0.9 0.9 %copy-done.1 = f32[4,32,256]{2,1,0:T(8,128)S(1)} copy-done((f32[4,32,256]{2,1,0:T(8,128)S(1)}, f32[4,32,256]{2,1,0:T(8,128)}, u32[]{:S(2)}) %copy-start.1) | copy-done | bytes 131096
  1.8 0.0 copy-start.2
  1.8 0.9 %copy-done.2 = f32[4,32,256]{2,1,0:T(8,128)S(1)} copy-done((f32[4,32,256]{2,1,0:T(8,128)S(1)}, f32[4,32,256]{2,1,0:T(8,128)}, u32[]{:S(2)}) %copy-start.2) | copy-done | bytes 131096
  2.7 0.0 copy-start.3
  2.7 0.9 %copy-done.3 = f32[4,32,256]{2,1,0:T(8,128)S(1)} copy-done((f32[4,32,256]{2,1,0:T(8,128)S(1)}, f32[4,32,256]{2,1,0:T(8,128)}, u32[]{:S(2)}) %copy-start.3) | copy-done | bytes 131096
  3.6 47.1 %cycle.1 = f32[4,32,256]{2,1,0:T(8,128)S(1)} custom-call(f32[4,32,256]{2,1,0:T(8,128)S(1)} %copy-done, f32[4,32,256]{2,1,0:T(8,128)S(1)} %copy-done.1, f32[4,32,256]{2,1,0:T(8,128)S(1)} %copy-done.2, f32[4,32,256]{2,1,0:T(8,128)S(1)} %copy-done.3), custom_call_target="tpu_custom_call" | custom-call | tf_op jit(solution)/shard_map/cycle/pallas_call | solution.py:358
  50.7 0.7 %copy.6 = f32[4,32,256]{2,1,0:T(8,128)} copy(f32[4,32,256]{2,1,0:T(8,128)S(1)} %cycle.1) | data formatting | bytes 262144
Async XLA Ops:
  0.0 0.9 %copy-start = (f32[4,32,256]{2,1,0:T(8,128)S(1)}, f32[4,32,256]{2,1,0:T(8,128)}, u32[]{:S(2)}) copy-start(f32[4,32,256]{2,1,0:T(8,128)} %source.1) | copy-start | bytes 393220
  0.9 0.9 %copy-start.1 = (f32[4,32,256]{2,1,0:T(8,128)S(1)}, f32[4,32,256]{2,1,0:T(8,128)}, u32[]{:S(2)}) copy-start(f32[4,32,256]{2,1,0:T(8,128)} %guess.1) | copy-start | bytes 393220
  1.8 0.9 %copy-start.2 = (f32[4,32,256]{2,1,0:T(8,128)S(1)}, f32[4,32,256]{2,1,0:T(8,128)}, u32[]{:S(2)}) copy-start(f32[4,32,256]{2,1,0:T(8,128)} %mass.1) | copy-start | bytes 393220
  2.7 0.9 %copy-start.3 = (f32[4,32,256]{2,1,0:T(8,128)S(1)}, f32[4,32,256]{2,1,0:T(8,128)}, u32[]{:S(2)}) copy-start(f32[4,32,256]{2,1,0:T(8,128)} %diff.1) | copy-start | bytes 393220

commit v2 on v1

v2 whole, which is shorter than its diff:
```python
import functools

import jax
import jax.numpy as jnp
from jax import lax
from jax.experimental import pallas as pl
from jax.experimental.pallas import tpu as pltpu
from jax.sharding import PartitionSpec as P

MESH = pl.DeviceIdType.MESH
CHEB_C = 8
FINE_LOW = 0.25
FINE_HIGH = 2.0
COARSE_LOW = 0.05
COARSE_HIGH = 2.0

FX0, FX1, FR0, FRN = 3, 7, 4, 32
CX0, CR0, CRN = 4, 4, 16
GUESS, DIFF, SOURCE, MASS = 0, 1, 2, 3

NEAR = [(i, j) for i in (-2, 2, -1, 1) for j in (-1, 1)] + [(-2, 0), (2, 0), (0, -1), (0, 1), (-1, 0), (1, 0)]
RING = [(i, j) for i in (-1, 1) for j in (-1, 1)] + [(0, -1), (0, 1), (-1, 0), (1, 0)]


def cheb_coeffs(count_steps, low_end, high_end):
    center_val = (high_end + low_end) / 2.0
    half_width = (high_end - low_end) / 2.0
    sigma_val = center_val / half_width
    factor_prev = 1.0 / sigma_val
    coeffs_list = [(0.0, 1.0 / center_val)]
    for number in range(1, count_steps):
        factor_next = 1.0 / (2.0 * sigma_val - factor_prev)
        coeffs_list.append((factor_next * factor_prev, 2.0 * factor_next / half_width))
        factor_prev = factor_next
    return coeffs_list


def coarse_rows(os):
    if os == 1:
        return pl.ds(CR0 + CRN - 4, 4), pl.ds(0, 4)
    if os == -1:
        return pl.ds(CR0, 4), pl.ds(CR0 + CRN, 4)
    return pl.ds(CR0, CRN), pl.ds(CR0, CRN)


def fine_cut(o, start, size, width):
    if o == 1:
        return pl.ds(start + size - width, width), pl.ds(start - width, width)
    if o == -1:
        return pl.ds(start, width), pl.ds(start + size, width)
    return pl.ds(start, size), pl.ds(start, size)


def rim_messages():
    own_x, own_rows, all_four = pl.ds(FX0, 4), pl.ds(FR0, FRN), pl.ds(0, 4)
    beside = []
    for j in (-1, 1):
        beside.append(((0, j), all_four, own_x, own_x) + fine_cut(j, FR0, FRN, 3))
    for i in (-1, 1):
        for j in (-1, 1):
            beside.append(((i, j), all_four) + fine_cut(i, FX0, 4, 2) + fine_cut(j, FR0, FRN, 2))
    ranks = []
    for depth in range(3):
        arrays = all_four if depth < 2 else pl.ds(0, 2)
        ranks.append([
            ((-1, 0), arrays, pl.ds(FX0 + depth, 1), pl.ds(FX1 + depth, 1), own_rows, own_rows),
            ((1, 0), arrays, pl.ds(FX1 - 1 - depth, 1), pl.ds(FX0 - 1 - depth, 1), own_rows, own_rows)])
    return [beside] + ranks


def dot(a, b):
    return jnp.dot(a, b, precision=lax.Precision.HIGHEST, preferred_element_type=jnp.float32)


def kernel(source, guess, mass, diff, out, F, FX, FY, FZ, DIAG, INV, W1, W2, DIR, RES, L2, C, G, A, B, XA, XB, CD,
           load_sem, r_send, r_recv, c_send, c_recv, e_send, e_recv, b_send, b_recv, l_send, l_recv):
    f32 = jnp.float32
    nbox, nsub = lax.axis_size("box"), lax.axis_size("sub")
    b, s = lax.axis_index("box"), lax.axis_index("sub")

    def both(p, q):
        return jnp.logical_and(p, q)

    def exists(o):
        box_in = {-2: b > 1, -1: b > 0, 0: None, 1: b < nbox - 1, 2: b < nbox - 2}[o[0]]
        sub_in = {-1: s > 0, 0: None, 1: s < nsub - 1}[o[1]]
        if box_in is None or sub_in is None:
            return sub_in if box_in is None else box_in
        return both(box_in, sub_in)

    inner = both(both(b > 1, b < nbox - 2), both(s > 0, s < nsub - 1))
    rim = jnp.logical_not(inner)

    def each(messages, act, back):
        @pl.when(inner)
        def _():
            for _, message in messages:
                act(message)

        @pl.when(rim)
        def _():
            for o, message in messages:
                pl.when(exists((-o[0], -o[1]) if back else o))(functools.partial(act, message))

    def start(messages):
        each(messages, lambda m: m.start(), False)

    def arrived(messages):
        each(messages, lambda m: m.wait_recv(), True)

    def left(messages):
        each(messages, lambda m: m.wait_send(), False)

    def message(o, src, dst, send, recv):
        return o, pltpu.make_async_remote_copy(
            src_ref=src, dst_ref=dst, send_sem=send, recv_sem=recv, device_id=(b + o[0], s + o[1]), device_id_type=MESH)

    loads = []
    for k, ref in enumerate((guess, diff, source, mass)):
        for h in range(2):
            loads.append(pltpu.make_async_copy(
                ref.at[:, :, pl.ds(128 * h, 128)], F.at[k, pl.ds(FX0, 4), h, pl.ds(FR0, FRN)], load_sem.at[k, h]))
            loads[-1].start()
    def outside(x_cut, row_cut, X_cut, coarse_row_cut, n_x, n_rows, n_X, n_coarse_rows):
        F[0:3, x_cut, :, row_cut] = jnp.zeros((3, n_x, 2, n_rows, 128), f32)
        F[3:4, x_cut, :, row_cut] = jnp.ones((1, n_x, 2, n_rows, 128), f32)
        L2[x_cut, :, row_cut] = jnp.zeros((n_x, 2, n_rows, 128), f32)
        C[:, X_cut, coarse_row_cut] = jnp.zeros((4, n_X, n_coarse_rows, 128), f32)
        A[X_cut, coarse_row_cut] = jnp.zeros((n_X, n_coarse_rows, 128), f32)
        B[:, X_cut, coarse_row_cut] = jnp.zeros((2, n_X, n_coarse_rows, 128), f32)

    def blank():
        every, lower, upper = slice(None), slice(0, 2), slice(8, 10)
        pl.when(b == 0)(lambda: outside(slice(0, FX0), every, slice(0, 4), every, FX0, 40, 4, 24))
        pl.when(b == nbox - 1)(lambda: outside(slice(FX1, 10), every, slice(6, 10), every, 10 - FX1, 40, 4, 24))
        pl.when(s == 0)(lambda: outside(every, slice(0, 4), every, slice(0, 4), 10, 4, 10, 4))
        pl.when(s == nsub - 1)(lambda: outside(every, slice(36, 40), every, slice(20, 24), 10, 4, 10, 4))

        @pl.when(b == 1)
        def _():
            C[:, lower] = jnp.zeros((4, 2, 24, 128), f32)
            A[lower] = jnp.zeros((2, 24, 128), f32)
            B[:, lower] = jnp.zeros((2, 2, 24, 128), f32)

        @pl.when(b == nbox - 2)
        def _():
            C[:, upper] = jnp.zeros((4, 2, 24, 128), f32)
            A[upper] = jnp.zeros((2, 24, 128), f32)
            B[:, upper] = jnp.zeros((2, 2, 24, 128), f32)

    barrier = pltpu.get_barrier_semaphore()

    def greet(o):
        pl.semaphore_signal(barrier, inc=1, device_id=(b + o[0], s + o[1]), device_id_type=MESH)

    for o in reversed(NEAR):
        pl.when(exists(o))(functools.partial(greet, o))
    pl.when(rim)(blank)
    for load in loads:
        load.wait()

    first, k = [], 0
    for group in rim_messages():
        first.append([])
        for o, arrays, xs, xd, rs, rd in group:
            first[-1].append(message(o, F.at[arrays, xs, :, rs], F.at[arrays, xd, :, rd], r_send.at[k], r_recv.at[k]))
            k += 1
    n_box = jnp.minimum(b, 2) + jnp.minimum(nbox - 1 - b, 2)
    n_sub = jnp.minimum(s, 1) + jnp.minimum(nsub - 1 - s, 1)
    pl.semaphore_wait(barrier, (n_box + 1) * (n_sub + 1) - 1)
    start([m for group in first for m in group])

    lane = lax.broadcasted_iota(jnp.int32, (256, 128), 0)
    cell = lax.broadcasted_iota(jnp.int32, (256, 128), 1)
    z_mean = jnp.where(lax.shift_right_logical(lane, 1) == cell, f32(0.5), f32(0.0))
    z_low = jnp.where(lax.shift_right_logical(lane + 1, 1) == cell, f32(0.5), f32(0.0))
    z_high = jnp.where(lax.shift_right_logical(lane + 1, 1) == cell + 1, f32(0.5), f32(0.0))
    row = lax.broadcasted_iota(jnp.int32, (2, 40, 128), 1)
    row_in = jnp.logical_and(jnp.logical_or(row >= FR0, s > 0), jnp.logical_or(row < FR0 + FRN, s < nsub - 1))
    row_mask = jnp.where(row_in, f32(1.0), f32(0.0))
    lane_f = lax.broadcasted_iota(jnp.int32, (2, 40, 128), 2)
    half = lax.broadcasted_iota(jnp.int32, (2, 40, 128), 0)
    z_first = jnp.logical_and(lane_f == 0, half == 0)
    z_last = jnp.logical_and(lane_f == 127, half == 1)

    def shift(v, edge, by):
        r = pltpu.roll(v, by, 2)
        return jnp.where(edge, jnp.stack([r[1], r[0]]), r)

    def from_below(v):
        return shift(v, lane_f == 0, 1)

    def from_above(v):
        return shift(v, lane_f == 127, 127)


    def slab_in(x):
        inside = jnp.logical_and(jnp.logical_or(x >= FX0, b > 0), jnp.logical_or(x < FX1, b < nbox - 1))
        return jnp.where(inside, f32(1.0), f32(0.0))

    def face(x):
        FX[x] = 0.5 * (F[DIFF, x - 1] + F[DIFF, x])

    def operator(x):
        d = F[DIFF, x]
        fy = 0.5 * (d + pltpu.roll(d, 1, 1))
        fz = 0.5 * (d + jnp.where(z_first, f32(0.0), from_below(d)))
        fz_high = 0.5 * (d + jnp.where(z_last, f32(0.0), from_above(d)))
        diag = F[MASS, x] + FX[x] + FX[x + 1] + fy + pltpu.roll(fy, 39, 1) + fz + fz_high
        FY[x] = fy
        FZ[x] = jnp.where(z_first, f32(0.0), fz)
        DIAG[x] = diag
        INV[x] = (row_mask * slab_in(x)) / diag

    def defect(u_ref, x):
        u = u_ref[x]
        fy, fz = FY[x], FZ[x]
        around = FX[x] * u_ref[x - 1] + FX[x + 1] * u_ref[x + 1]
        around = around + fy * pltpu.roll(u, 1, 1) + pltpu.roll(fy * u, 39, 1)
        around = around + fz * from_below(u) + from_above(fz * u)
        return (F[SOURCE, x] - DIAG[x] * u) + around, u

    fine = cheb_coeffs(2, FINE_LOW, FINE_HIGH)
    coarse = cheb_coeffs(CHEB_C, COARSE_LOW, COARSE_HIGH)

    def first_step(u_ref, to_ref, x):
        c, u = defect(u_ref, x)
        step_dir = (fine[0][1] * INV[x]) * c
        DIR[x] = step_dir
        to_ref[x] = u + step_dir

    def second_step(x):
        c, u = defect(W1, x)
        return u + (fine[1][0] * DIR[x] + (fine[1][1] * INV[x]) * c)

    def over(lo, hi, work, step=1):
        def turn(k, carry):
            work(lo + step * k)
            return carry

        lax.fori_loop(0, (hi - lo + step - 1) // step, turn, 0)

    def with_operator(x):
        operator(x)
        first_step(F.at[GUESS], W1, x)

    def smooth(x):
        W2[x] = second_step(x)

    def find_residual(x):
        RES[x] = defect(W2, x)[0]

    arrived(first[0])
    over(4, 7, face)
    with jax.named_scope("rank_one"):
        arrived(first[1])
    with jax.named_scope("work_one"):
        over(3, 8, face, 4)
        over(3, 7, with_operator)
    with jax.named_scope("coarse_coefficients"):
        def rows(ref, x, start):
            return ref[x, :, pl.ds(start, 16, 2), :]

        def wide(parts):
            return jnp.concatenate([jnp.concatenate([v[0], v[1]], 1) for v in parts], 0)


        D, M = F.at[DIFF], F.at[MASS]
        pair = {x: rows(D, x, FR0) + rows(D, x, FR0 + 1) for x in range(FX0 - 1, FX1 + 1)}
        low_y = {x: rows(D, x, FR0 - 1) + rows(D, x, FR0) for x in range(FX0, FX1)}
        high_y = {x: rows(D, x, FR0 + 1) + rows(D, x, FR0 + 2) for x in range(FX0, FX1)}
        in_mean, in_z = [], []
        for X in range(2):
            x = FX0 + 2 * X
            face_low, face_high = 0.25 * (pair[x - 1] + pair[x]), 0.25 * (pair[x + 1] + pair[x + 2])
            y_low, y_high = 0.25 * (low_y[x] + low_y[x + 1]), 0.25 * (high_y[x] + high_y[x + 1])
            mean_mass = 0.25 * (rows(M, x, FR0) + rows(M, x, FR0 + 1) + rows(M, x + 1, FR0) + rows(M, x + 1, FR0 + 1))
            in_mean += [face_low, y_low, mean_mass + 0.25 * (face_low + face_high + y_low + y_high)]
            in_z.append(0.25 * (pair[x] + pair[x + 1]))
        means = dot(wide(in_mean), z_mean)
        over_z = wide(in_z)
        lows_z, highs_z = dot(over_z, z_low), dot(over_z, z_high)
        own_s = []
        for X in range(2):
            fx, fy, d = (means[(3 * X + k) * 16:(3 * X + k + 1) * 16] for k in range(3))
            fz = lows_z[16 * X:16 * X + 16]
            d = d + 0.25 * (fz + highs_z[16 * X:16 * X + 16])
            sc = lax.rsqrt(d)
            sc = sc * (1.5 - 0.5 * d * sc * sc)
            own_s.append(sc)
            for k, v in enumerate((fx, fy, fz, sc)):
                C[k, CX0 + X, pl.ds(CR0, CRN), :] = v

    def coarse_messages(src, lead, sends, recvs):
        found = []
        for k, o in enumerate(NEAR):
            rs, rd = coarse_rows(o[1])
            found.append(message(
                o, src.at[lead + (pl.ds(CX0, 2), rs)], src.at[lead + (pl.ds(CX0 - 2 * o[0], 2), rd)], sends.at[k], recvs.at[k]))
        start(found)
        return found

    with jax.named_scope("rank_two"):
        arrived(first[2])
    with jax.named_scope("work_two"):
        over(2, 9, face, 6)
        over(2, 8, with_operator, 5)
        over(3, 7, smooth)
    coefs = coarse_messages(C, (pl.ds(0, 4),), c_send, c_recv)
    with jax.named_scope("rank_three"):
        arrived(first[3])
    with jax.named_scope("work_three"):
        over(1, 10, face, 8)
        over(1, 9, with_operator, 7)
        over(2, 8, smooth, 5)
        over(FX0, FX1, find_residual)

    means = []
    for X in range(2):
        x = FX0 + 2 * X
        means.append(0.25 * ((rows(RES, x, FR0) + rows(RES, x, FR0 + 1)) + (rows(RES, x + 1, FR0) + rows(RES, x + 1, FR0 + 1))))
    rhs = dot(wide(means), z_mean)
    for X in range(2):
        A[CX0 + X, pl.ds(CR0, CRN), :] = own_s[X] * rhs[16 * X:16 * X + 16]
    e_one = coarse_messages(A, (), e_send, e_recv)

    for x in range(FX0, FX1):
        L2[x, :, pl.ds(FR0, FRN), :] = W2[x, :, pl.ds(FR0, FRN), :]
    late = []
    for k, o in enumerate(RING):
        xs, xd = fine_cut(o[0], FX0, 4, 2)
        rs, rd = fine_cut(o[1], FR0, FRN, 2)
        late.append(message(o, L2.at[xs, :, rs], L2.at[xd, :, rd], l_send.at[k], l_recv.at[k]))
    start(late)

    with jax.named_scope("wait_coefficients"):
        arrived(coefs)
    clane = lax.broadcasted_iota(jnp.int32, (24, 128), 1)
    for X in range(10):
        sc = C[3, X]
        if X > 0:
            G[0, X] = C[0, X] * ((0.25 * sc) * C[3, X - 1])
        G[1, X] = C[1, X] * ((0.25 * sc) * pltpu.roll(sc, 1, 0))
        G[2, X] = jnp.where(clane == 0, f32(0.0), C[2, X] * ((0.25 * sc) * pltpu.roll(sc, 1, 1)))

    def coarse_step(x_ref, d_ref, to_x, to_d, X, number):
        keep, gain = coarse[number]
        x = x_ref[X]
        gy, gz = G[1, X], G[2, X]
        c = (A[X] - x) + G[0, X] * x_ref[X - 1] + G[0, X + 1] * x_ref[X + 1]
        c = c + gy * pltpu.roll(x, 1, 0) + pltpu.roll(gy * x, 23, 0)
        c = c + gz * pltpu.roll(x, 1, 1) + pltpu.roll(gz * x, 127, 1)
        step_dir = keep * d_ref[X] + gain * c
        return x + step_dir, step_dir

    with jax.named_scope("wait_right_hand_side"):
        left([m for group in first for m in group])
        arrived(e_one)
    for X in range(10):
        begin = coarse[0][1] * A[X]
        XA[X] = begin
        CD[X] = begin
    now, later = XA, XB
    for number in range(1, 4):
        for X in range(number, 10 - number):
            later[X], CD[X] = coarse_step(now, CD, None, None, X, number)
        now, later = later, now
    for X in range(CX0, CX0 + 2):
        new_x, new_d = coarse_step(now, CD, None, None, X, 4)
        B[0, X, pl.ds(CR0, CRN), :] = new_x[CR0:CR0 + CRN]
        B[1, X, pl.ds(CR0, CRN), :] = new_d[CR0:CR0 + CRN]
    e_two = coarse_messages(B, (pl.ds(0, 2),), b_send, b_recv)
    with jax.named_scope("wait_iterate"):
        left(coefs + e_one)
        arrived(late)
        left(late)
        arrived(e_two)
    now, now_d = B.at[0], B.at[1]
    for number, later in ((5, XA), (6, XB), (7, XA)):
        for X in range(number - 4, 14 - number):
            later[X], CD[X] = coarse_step(now, now_d, None, None, X, number)
        now, now_d = later, CD

    spread_z = jnp.where(
        lax.shift_right_logical(lax.broadcasted_iota(jnp.int32, (128, 256), 1), 1) == lax.broadcasted_iota(jnp.int32, (128, 256), 0),
        f32(1.0), f32(0.0))
    spread_y = jnp.where(
        lax.shift_right_logical(lax.broadcasted_iota(jnp.int32, (40, 24), 0) + (2 * CR0 - FR0), 1) == lax.broadcasted_iota(jnp.int32, (40, 24), 1),
        f32(1.0), f32(0.0))
    corr = jnp.concatenate([C[3, X] * now[X] for X in range(3, 7)], 0)
    corr = dot(corr, spread_z)
    for X in range(4):
        fine_corr = dot(spread_y, corr[24 * X:24 * X + 24])
        fine_corr = jnp.stack([fine_corr[:, :128], fine_corr[:, 128:]])
        for x in (2 * X + 1, 2 * X + 2):
            W2[x] = L2[x] + fine_corr

    over(2, 8, functools.partial(first_step, W2, W1))
    for x in range(FX0, FX1):
        last = second_step(x)
        for h in range(2):
            out[x - FX0, :, 128 * h:128 * h + 128] = last[h, FR0:FR0 + FRN]

    left(e_two)


def body(source, guess, mass_coef, diffusion):
    vmem = pltpu.VMEM
    fine_slabs = lambda: vmem((10, 2, 40, 128), jnp.float32)
    coarse_slabs = lambda: vmem((10, 24, 128), jnp.float32)
    n_rim, n_near, n_ring = sum(len(group) for group in rim_messages()), len(NEAR), len(RING)
    dma = pltpu.SemaphoreType.DMA
    return pl.pallas_call(
        kernel,
        out_shape=jax.ShapeDtypeStruct((4, 32, 256), jnp.float32),
        in_specs=[pl.BlockSpec(memory_space=pltpu.HBM)] * 4,
        out_specs=pl.BlockSpec(memory_space=pltpu.VMEM),
        scratch_shapes=[
            vmem((4, 10, 2, 40, 128), jnp.float32),
            fine_slabs(), fine_slabs(), fine_slabs(), fine_slabs(), fine_slabs(),
            fine_slabs(), fine_slabs(), fine_slabs(), fine_slabs(), fine_slabs(),
            vmem((4, 10, 24, 128), jnp.float32),
            vmem((3, 10, 24, 128), jnp.float32),
            coarse_slabs(),
            vmem((2, 10, 24, 128), jnp.float32),
            coarse_slabs(), coarse_slabs(), coarse_slabs(),
            dma((4, 2)),
            dma((n_rim,)), dma((n_rim,)),
            dma((n_near,)), dma((n_near,)),
            dma((n_near,)), dma((n_near,)),
            dma((n_near,)), dma((n_near,)),
            dma((n_ring,)), dma((n_ring,)),
        ],
        compiler_params=pltpu.CompilerParams(collective_id=0, has_side_effects=True, vmem_limit_bytes=63 * 2**20),
        name="cycle",
    )(source, guess, mass_coef, diffusion)


def solution(mesh):
    spec = P("box", "sub", None)
    return jax.shard_map(body, mesh=mesh, in_specs=(spec,) * 4, out_specs=spec, check_vma=False)
```

time: 51.6 us -> 35.9 us (0.70)
  Pallas kernels: 47.1 us -> 34.1 us
  local copies, waits for them, and re-layouts: 4.27 us -> 1.57 us
    pallas_call x1, Pallas kernels: 47.1 us -> 34.1 us  [body(): pl.pallas_call(kernel, out_shape=jax.ShapeDtypeStruct((4, 32, 256), jnp.f...]
    unnamed x9 -> x1, local copies, waits for them, and re-layouts: 4.27 us -> 1.57 us
where the time goes in v2:
time: 35.9 us; the launch traced here: 35.7 us
  Pallas kernels  34.1 us (95%)
  local copies, waits for them, and re-layouts  1.57 us (4%)
    pallas_call x1, Pallas kernels, body(): pl.pallas_call(kernel, out_shape=jax.ShapeDtypeStruct((4, 32, 256), jnp.f...  34.1 us
    unnamed x1, local copies, waits for them, and re-layouts  1.57 us

profile of v2, /device:TPU:1, one launch (start us, length us, event | category | flops | bytes accessed | tf_op | source)
XLA Modules:
  0.0 35.7 jit_solution(2274556078043192763)
XLA Ops:
  0.0 34.1 %cycle.1 = f32[4,32,256]{2,1,0:T(8,128)} custom-call(f32[4,32,256]{2,1,0:T(8,128)} %source.1, f32[4,32,256]{2,1,0:T(8,128)} %guess.1, f32[4,32,256]{2,1,0:T(8,128)} %mass.1, f32[4,32,256]{2,1,0:T(8,128)} %diff.1), custom_call_target="tpu_custom_call" | custom-call | tf_op jit(solution)/shard_map/cycle/pallas_call | solution.py:413
  34.1 1.6 %copy.6 = f32[4,32,256]{2,1,0:T(8,128)} copy(f32[4,32,256]{2,1,0:T(8,128)} %cycle.1) | data formatting | bytes 262144

commit v3 on v2

--- a/solution.py
+++ b/solution.py
@@ -19,6 +19,7 @@
 GUESS, DIFF, SOURCE, MASS = 0, 1, 2, 3
 
 NEAR = [(i, j) for i in (-2, 2, -1, 1) for j in (-1, 1)] + [(-2, 0), (2, 0), (0, -1), (0, 1), (-1, 0), (1, 0)]
+PLUS = [(0, 1), (1, -1), (1, 0), (1, 1), (2, -1), (2, 0), (2, 1)]
 RING = [(i, j) for i in (-1, 1) for j in (-1, 1)] + [(0, -1), (0, 1), (-1, 0), (1, 0)]
 
 
@@ -73,7 +74,7 @@
 
 
 def kernel(source, guess, mass, diff, out, F, FX, FY, FZ, DIAG, INV, W1, W2, DIR, RES, L2, C, G, A, B, XA, XB, CD,
-           load_sem, r_send, r_recv, c_send, c_recv, e_send, e_recv, b_send, b_recv, l_send, l_recv):
+           load_sem, r_send, r_recv, c_send, c_recv, e_send, e_recv, b_send, b_recv, l_send, l_recv, ready):
     f32 = jnp.float32
     nbox, nsub = lax.axis_size("box"), lax.axis_size("sub")
     b, s = lax.axis_index("box"), lax.axis_index("sub")
@@ -115,6 +116,16 @@
         return o, pltpu.make_async_remote_copy(
             src_ref=src, dst_ref=dst, send_sem=send, recv_sem=recv, device_id=(b + o[0], s + o[1]), device_id_type=MESH)
 
+    barrier = pltpu.get_barrier_semaphore()
+
+    def greet(o, semaphore):
+        pl.semaphore_signal(semaphore, inc=1, device_id=(b + o[0], s + o[1]), device_id_type=MESH)
+
+    def minus(o):
+        return (-o[0], -o[1])
+
+    for o in PLUS:
+        pl.when(exists(minus(o)))(functools.partial(greet, minus(o), barrier))
     loads = []
     for k, ref in enumerate((guess, diff, source, mass)):
         for h in range(2):
@@ -148,14 +159,6 @@
             A[upper] = jnp.zeros((2, 24, 128), f32)
             B[:, upper] = jnp.zeros((2, 2, 24, 128), f32)
 
-    barrier = pltpu.get_barrier_semaphore()
-
-    def greet(o):
-        pl.semaphore_signal(barrier, inc=1, device_id=(b + o[0], s + o[1]), device_id_type=MESH)
-
-    for o in reversed(NEAR):
-        pl.when(exists(o))(functools.partial(greet, o))
-    pl.when(rim)(blank)
     for load in loads:
         load.wait()
 
@@ -165,10 +168,22 @@
         for o, arrays, xs, xd, rs, rd in group:
             first[-1].append(message(o, F.at[arrays, xs, :, rs], F.at[arrays, xd, :, rd], r_send.at[k], r_recv.at[k]))
             k += 1
-    n_box = jnp.minimum(b, 2) + jnp.minimum(nbox - 1 - b, 2)
+    n_box = jnp.minimum(nbox - 1 - b, 2)
     n_sub = jnp.minimum(s, 1) + jnp.minimum(nsub - 1 - s, 1)
-    pl.semaphore_wait(barrier, (n_box + 1) * (n_sub + 1) - 1)
-    start([m for group in first for m in group])
+    n_plus = n_box * (n_sub + 1) + jnp.minimum(nsub - 1 - s, 1)
+    pl.when(n_plus > 0)(lambda: pl.semaphore_wait(barrier, n_plus))
+    for k, o in enumerate(PLUS):
+        pl.when(exists(o))(functools.partial(greet, o, ready.at[k]))
+    flat = [m for group in first for m in group]
+    start([m for m in flat if m[0] in PLUS])
+
+    def met(o):
+        pl.when(exists(minus(o)))(lambda: pl.semaphore_wait(ready.at[PLUS.index(o)], 1))
+
+    for o in ((1, -1), (0, 1), (1, 0), (1, 1)):
+        met(o)
+        start([m for m in flat if m[0] == minus(o)])
+    pl.when(rim)(blank)
 
     lane = lax.broadcasted_iota(jnp.int32, (256, 128), 0)
     cell = lax.broadcasted_iota(jnp.int32, (256, 128), 1)
@@ -238,7 +253,7 @@
             work(lo + step * k)
             return carry
 
-        lax.fori_loop(0, (hi - lo + step - 1) // step, turn, 0)
+        lax.fori_loop(0, (hi - lo + step - 1) // step, turn, 0, unroll=True)
 
     def with_operator(x):
         operator(x)
@@ -306,6 +321,8 @@
         over(2, 9, face, 6)
         over(2, 8, with_operator, 5)
         over(3, 7, smooth)
+    for o in PLUS[4:]:
+        met(o)
     coefs = coarse_messages(C, (pl.ds(0, 4),), c_send, c_recv)
     with jax.named_scope("rank_three"):
         arrived(first[3])
@@ -354,7 +371,7 @@
         return x + step_dir, step_dir
 
     with jax.named_scope("wait_right_hand_side"):
-        left([m for group in first for m in group])
+        left(flat)
         arrived(e_one)
     for X in range(10):
         begin = coarse[0][1] * A[X]
@@ -430,10 +447,11 @@
             dma((n_near,)), dma((n_near,)),
             dma((n_near,)), dma((n_near,)),
             dma((n_ring,)), dma((n_ring,)),
+            pltpu.SemaphoreType.REGULAR((len(PLUS),)),
         ],
-        compiler_params=pltpu.CompilerParams(collective_id=0, has_side_effects=True, vmem_limit_bytes=63 * 2**20),
+        compiler_params=pltpu.CompilerParams(collective_id=0, has_side_effects=True, vmem_limit_bytes=48 * 2**20),
         name="cycle",
-    )(source, guess, mass_coef, diffusion)
+    )(*[pltpu.with_memory_space_constraint(v, pltpu.HBM) for v in (source, guess, mass_coef, diffusion)])
 
 
 def solution(mesh):

time: 35.9 us -> 32.6 us (0.908)
  Pallas kernels: 34.1 us -> 31.7 us
  local copies, waits for them, and re-layouts: 1.57 us -> 0.66 us
    pallas_call x1, Pallas kernels: 34.1 us -> 31.7 us  [body(): pl.pallas_call(kernel, out_shape=jax.ShapeDtypeStruct((4, 32, 256), jnp.f...]
    unnamed x1, local copies, waits for them, and re-layouts: 1.57 us -> 0.66 us
where the time goes in v3:
time: 32.6 us; the launch traced here: 32.4 us
  Pallas kernels  31.7 us (97%)
  local copies, waits for them, and re-layouts  0.66 us (2%)
    pallas_call x1, Pallas kernels, body(): pl.pallas_call(kernel, out_shape=jax.ShapeDtypeStruct((4, 32, 256), jnp.f...  31.7 us
    unnamed x1, local copies, waits for them, and re-layouts  0.66 us

profile of v3, /device:TPU:1, one launch (start us, length us, event | category | flops | bytes accessed | tf_op | source)
XLA Modules:
  0.0 32.4 jit_solution(11744012343320877531)
XLA Ops:
  0.0 31.7 %cycle.1 = f32[4,32,256]{2,1,0:T(8,128)S(1)} custom-call(f32[4,32,256]{2,1,0:T(8,128)} %source.1, f32[4,32,256]{2,1,0:T(8,128)} %guess.1, f32[4,32,256]{2,1,0:T(8,128)} %mass.1, f32[4,32,256]{2,1,0:T(8,128)} %diff.1), custom_call_target="tpu_custom_call" | custom-call | tf_op jit(solution)/shard_map/cycle/pallas_call | solution.py:430
  31.7 0.7 %copy.6 = f32[4,32,256]{2,1,0:T(8,128)} copy(f32[4,32,256]{2,1,0:T(8,128)S(1)} %cycle.1) | data formatting | bytes 262144

commit v4 on v3

--- a/solution.py
+++ b/solution.py
@@ -20,6 +20,9 @@
 
 NEAR = [(i, j) for i in (-2, 2, -1, 1) for j in (-1, 1)] + [(-2, 0), (2, 0), (0, -1), (0, 1), (-1, 0), (1, 0)]
 PLUS = [(0, 1), (1, -1), (1, 0), (1, 1), (2, -1), (2, 0), (2, 1)]
+LOW_Y, LOW_Z, LOW_X, ROOT = (0, 6), (1, 7), (2, 5), (3, 4)
+C_SLOTS, A_SLOTS, B_SLOTS = 8, 2, 4
+STEP, ITERATE = (0, 3), (1, 2)
 RING = [(i, j) for i in (-1, 1) for j in (-1, 1)] + [(0, -1), (0, 1), (-1, 0), (1, 0)]
 
 
@@ -36,12 +39,26 @@
     return coeffs_list
 
 
-def coarse_rows(os):
+def coarse_rows(os, width):
     if os == 1:
-        return pl.ds(CR0 + CRN - 4, 4), pl.ds(0, 4)
+        return pl.ds(CR0 + CRN - width, width), pl.ds(CR0 - width, width)
     if os == -1:
-        return pl.ds(CR0, 4), pl.ds(CR0 + CRN, 4)
+        return pl.ds(CR0, width), pl.ds(CR0 + CRN, width)
     return pl.ds(CR0, CRN), pl.ds(CR0, CRN)
+
+
+def coef_cut(o):
+    return {2: (3, 5), -2: (0, 6)}.get(o[0], (0, C_SLOTS)) + (2 if abs(o[0]) == 2 else 4,)
+
+
+def rhs_cut(o):
+    if abs(o[0]) == 2 and o[1] != 0:
+        return (1 if o[0] == 2 else 0), 1, 1
+    return 0, A_SLOTS, (4 if o[0] == 0 else 3)
+
+
+def iterate_cut(o):
+    return {2: (1, 3), -2: (0, 3)}.get(o[0], (0, B_SLOTS)) + (2 if abs(o[0]) == 2 else 4,)
 
 
 def fine_cut(o, start, size, width):
@@ -124,8 +141,20 @@
     def minus(o):
         return (-o[0], -o[1])
 
+    origin = both(b == 0, s == 0)
+    other = jnp.logical_not(origin)
+
+    def is_origin(o):
+        return both(b + o[0] == 0, s + o[1] == 0)
+
+    def there(o):
+        return both(exists(o), jnp.logical_not(is_origin(o)))
+
+    MINUS = [minus(o) for o in PLUS]
     for o in PLUS:
-        pl.when(exists(minus(o)))(functools.partial(greet, minus(o), barrier))
+        pl.when(both(exists(o), other))(functools.partial(greet, o, barrier))
+    for o in MINUS:
+        pl.when(is_origin(o))(functools.partial(greet, o, barrier))
     loads = []
     for k, ref in enumerate((guess, diff, source, mass)):
         for h in range(2):
@@ -136,28 +165,20 @@
         F[0:3, x_cut, :, row_cut] = jnp.zeros((3, n_x, 2, n_rows, 128), f32)
         F[3:4, x_cut, :, row_cut] = jnp.ones((1, n_x, 2, n_rows, 128), f32)
         L2[x_cut, :, row_cut] = jnp.zeros((n_x, 2, n_rows, 128), f32)
-        C[:, X_cut, coarse_row_cut] = jnp.zeros((4, n_X, n_coarse_rows, 128), f32)
-        A[X_cut, coarse_row_cut] = jnp.zeros((n_X, n_coarse_rows, 128), f32)
-        B[:, X_cut, coarse_row_cut] = jnp.zeros((2, n_X, n_coarse_rows, 128), f32)
+        blank_coarse(X_cut, coarse_row_cut, n_X, n_coarse_rows)
+
+    def blank_coarse(group_cut, row_cut, n_groups, n_rows):
+        for ref, slots in ((C, C_SLOTS), (A, A_SLOTS), (B, B_SLOTS)):
+            ref[group_cut, :, row_cut] = jnp.zeros((n_groups, slots, n_rows, 128), f32)
 
     def blank():
-        every, lower, upper = slice(None), slice(0, 2), slice(8, 10)
-        pl.when(b == 0)(lambda: outside(slice(0, FX0), every, slice(0, 4), every, FX0, 40, 4, 24))
-        pl.when(b == nbox - 1)(lambda: outside(slice(FX1, 10), every, slice(6, 10), every, 10 - FX1, 40, 4, 24))
-        pl.when(s == 0)(lambda: outside(every, slice(0, 4), every, slice(0, 4), 10, 4, 10, 4))
-        pl.when(s == nsub - 1)(lambda: outside(every, slice(36, 40), every, slice(20, 24), 10, 4, 10, 4))
-
-        @pl.when(b == 1)
-        def _():
-            C[:, lower] = jnp.zeros((4, 2, 24, 128), f32)
-            A[lower] = jnp.zeros((2, 24, 128), f32)
-            B[:, lower] = jnp.zeros((2, 2, 24, 128), f32)
-
-        @pl.when(b == nbox - 2)
-        def _():
-            C[:, upper] = jnp.zeros((4, 2, 24, 128), f32)
-            A[upper] = jnp.zeros((2, 24, 128), f32)
-            B[:, upper] = jnp.zeros((2, 2, 24, 128), f32)
+        every = slice(None)
+        pl.when(b == 0)(lambda: outside(slice(0, FX0), every, slice(0, 2), every, FX0, 40, 2, 24))
+        pl.when(b == nbox - 1)(lambda: outside(slice(FX1, 10), every, slice(3, 5), every, 10 - FX1, 40, 2, 24))
+        pl.when(s == 0)(lambda: outside(every, slice(0, 4), every, slice(0, 4), 10, 4, 5, 4))
+        pl.when(s == nsub - 1)(lambda: outside(every, slice(36, 40), every, slice(20, 24), 10, 4, 5, 4))
+        pl.when(b == 1)(lambda: blank_coarse(slice(0, 1), every, 1, 24))
+        pl.when(b == nbox - 2)(lambda: blank_coarse(slice(4, 5), every, 1, 24))
 
     for load in loads:
         load.wait()
@@ -168,21 +189,44 @@
         for o, arrays, xs, xd, rs, rd in group:
             first[-1].append(message(o, F.at[arrays, xs, :, rs], F.at[arrays, xd, :, rd], r_send.at[k], r_recv.at[k]))
             k += 1
-    n_box = jnp.minimum(nbox - 1 - b, 2)
+    flat = [m for group in first for m in group]
     n_sub = jnp.minimum(s, 1) + jnp.minimum(nsub - 1 - s, 1)
-    n_plus = n_box * (n_sub + 1) + jnp.minimum(nsub - 1 - s, 1)
-    pl.when(n_plus > 0)(lambda: pl.semaphore_wait(barrier, n_plus))
-    for k, o in enumerate(PLUS):
-        pl.when(exists(o))(functools.partial(greet, o, ready.at[k]))
-    flat = [m for group in first for m in group]
-    start([m for m in flat if m[0] in PLUS])
-
-    def met(o):
-        pl.when(exists(minus(o)))(lambda: pl.semaphore_wait(ready.at[PLUS.index(o)], 1))
-
-    for o in ((1, -1), (0, 1), (1, 0), (1, 1)):
-        met(o)
-        start([m for m in flat if m[0] == minus(o)])
+    n_minus = jnp.minimum(b, 2) * (n_sub + 1) + jnp.minimum(s, 1)
+    n_plus = jnp.minimum(nbox - 1 - b, 2) * (n_sub + 1) + jnp.minimum(nsub - 1 - s, 1)
+    by_origin = both(both(b < 3, s < 2), other)
+
+    def wait_barrier(count):
+        pl.when(count > 0)(lambda: pl.semaphore_wait(barrier, count))
+
+    pl.when(origin)(lambda: wait_barrier(n_plus))
+    pl.when(by_origin)(lambda: wait_barrier(n_minus - 1))
+    pl.when(jnp.logical_not(jnp.logical_or(origin, by_origin)))(lambda: wait_barrier(n_minus))
+
+    def slot(o):
+        return ready.at[NEAR.index(o)]
+
+    for o in MINUS:
+        pl.when(there(o))(functools.partial(greet, o, slot(minus(o))))
+    for o in PLUS:
+        pl.when(both(exists(o), origin))(functools.partial(greet, o, slot(minus(o))))
+
+    def send(o):
+        for m in flat:
+            if m[0] == o:
+                m[1].start()
+
+    def send_met(o):
+        pl.semaphore_wait(slot(o), 1)
+        send(o)
+
+    for o in MINUS[:4]:
+        pl.when(there(o))(functools.partial(send, o))
+    for o in PLUS[:4]:
+        pl.when(both(exists(o), origin))(functools.partial(send, o))
+    for o in PLUS[:4]:
+        pl.when(both(exists(o), other))(functools.partial(send_met, o))
+    for o in MINUS[:4]:
+        pl.when(is_origin(o))(functools.partial(send_met, o))
     pl.when(rim)(blank)
 
     lane = lax.broadcasted_iota(jnp.int32, (256, 128), 0)
@@ -269,9 +313,6 @@
     over(4, 7, face)
     with jax.named_scope("rank_one"):
         arrived(first[1])
-    with jax.named_scope("work_one"):
-        over(3, 8, face, 4)
-        over(3, 7, with_operator)
     with jax.named_scope("coarse_coefficients"):
         def rows(ref, x, start):
             return ref[x, :, pl.ds(start, 16, 2), :]
@@ -303,27 +344,37 @@
             sc = lax.rsqrt(d)
             sc = sc * (1.5 - 0.5 * d * sc * sc)
             own_s.append(sc)
-            for k, v in enumerate((fx, fy, fz, sc)):
-                C[k, CX0 + X, pl.ds(CR0, CRN), :] = v
-
-    def coarse_messages(src, lead, sends, recvs):
+            for kind, v in ((LOW_X, fx), (LOW_Y, fy), (LOW_Z, fz), (ROOT, sc)):
+                C[2, kind[X], pl.ds(CR0, CRN), :] = v
+
+    def coarse_messages(src, cut, sends, recvs):
         found = []
         for k, o in enumerate(NEAR):
-            rs, rd = coarse_rows(o[1])
+            at, count, width = cut(o)
+            rs, rd = coarse_rows(o[1], width)
             found.append(message(
-                o, src.at[lead + (pl.ds(CX0, 2), rs)], src.at[lead + (pl.ds(CX0 - 2 * o[0], 2), rd)], sends.at[k], recvs.at[k]))
+                o, src.at[2, pl.ds(at, count), rs], src.at[2 - o[0], pl.ds(at, count), rd], sends.at[k], recvs.at[k]))
         start(found)
         return found
 
+    def meet(o):
+        pl.semaphore_wait(slot(o), 1)
+
+    for o in PLUS[4:]:
+        pl.when(both(exists(o), other))(functools.partial(meet, o))
+    for o in MINUS[4:]:
+        pl.when(is_origin(o))(functools.partial(meet, o))
+    coefs = coarse_messages(C, coef_cut, c_send, c_recv)
+
+    with jax.named_scope("work_one"):
+        over(3, 8, face, 4)
+        over(3, 7, with_operator)
     with jax.named_scope("rank_two"):
         arrived(first[2])
     with jax.named_scope("work_two"):
         over(2, 9, face, 6)
         over(2, 8, with_operator, 5)
         over(3, 7, smooth)
-    for o in PLUS[4:]:
-        met(o)
-    coefs = coarse_messages(C, (pl.ds(0, 4),), c_send, c_recv)
     with jax.named_scope("rank_three"):
         arrived(first[3])
     with jax.named_scope("work_three"):
@@ -338,65 +389,77 @@
         means.append(0.25 * ((rows(RES, x, FR0) + rows(RES, x, FR0 + 1)) + (rows(RES, x + 1, FR0) + rows(RES, x + 1, FR0 + 1))))
     rhs = dot(wide(means), z_mean)
     for X in range(2):
-        A[CX0 + X, pl.ds(CR0, CRN), :] = own_s[X] * rhs[16 * X:16 * X + 16]
-    e_one = coarse_messages(A, (), e_send, e_recv)
-
-    for x in range(FX0, FX1):
+        A[2, X, pl.ds(CR0, CRN), :] = own_s[X] * rhs[16 * X:16 * X + 16]
+    e_one = coarse_messages(A, rhs_cut, e_send, e_recv)
+
+    for x in range(FX0 - 1, FX1 + 1):
         L2[x, :, pl.ds(FR0, FRN), :] = W2[x, :, pl.ds(FR0, FRN), :]
     late = []
     for k, o in enumerate(RING):
-        xs, xd = fine_cut(o[0], FX0, 4, 2)
-        rs, rd = fine_cut(o[1], FR0, FRN, 2)
+        if o[1] == 0:
+            at_x = FX1 - 2 if o[0] == 1 else FX0 + 1
+            xs, xd = pl.ds(at_x, 1), pl.ds(at_x - 4 * o[0], 1)
+        else:
+            xs, xd = fine_cut(o[0], FX0, 4, 1)
+        rs, rd = fine_cut(o[1], FR0, FRN, 2 if o[0] == 0 else 1)
         late.append(message(o, L2.at[xs, :, rs], L2.at[xd, :, rd], l_send.at[k], l_recv.at[k]))
     start(late)
 
     with jax.named_scope("wait_coefficients"):
         arrived(coefs)
     clane = lax.broadcasted_iota(jnp.int32, (24, 128), 1)
-    for X in range(10):
-        sc = C[3, X]
-        if X > 0:
-            G[0, X] = C[0, X] * ((0.25 * sc) * C[3, X - 1])
-        G[1, X] = C[1, X] * ((0.25 * sc) * pltpu.roll(sc, 1, 0))
-        G[2, X] = jnp.where(clane == 0, f32(0.0), C[2, X] * ((0.25 * sc) * pltpu.roll(sc, 1, 1)))
-
-    def coarse_step(x_ref, d_ref, to_x, to_d, X, number):
+
+    def coef(kind, X):
+        return C[X // 2, kind[X % 2]]
+
+    for X in range(1, 10):
+        sc = coef(ROOT, X)
+        G[0, X] = coef(LOW_X, X) * ((0.25 * sc) * coef(ROOT, X - 1))
+        if X < 9:
+            G[1, X] = coef(LOW_Y, X) * ((0.25 * sc) * pltpu.roll(sc, 1, 0))
+            G[2, X] = jnp.where(clane == 0, f32(0.0), coef(LOW_Z, X) * ((0.25 * sc) * pltpu.roll(sc, 1, 1)))
+
+    def coarse_step(iterate, step_of, X, number):
         keep, gain = coarse[number]
-        x = x_ref[X]
+        x = iterate(X)
         gy, gz = G[1, X], G[2, X]
-        c = (A[X] - x) + G[0, X] * x_ref[X - 1] + G[0, X + 1] * x_ref[X + 1]
+        c = (A[X // 2, X % 2] - x) + G[0, X] * iterate(X - 1) + G[0, X + 1] * iterate(X + 1)
         c = c + gy * pltpu.roll(x, 1, 0) + pltpu.roll(gy * x, 23, 0)
         c = c + gz * pltpu.roll(x, 1, 1) + pltpu.roll(gz * x, 127, 1)
-        step_dir = keep * d_ref[X] + gain * c
+        step_dir = keep * step_of(X) + gain * c
         return x + step_dir, step_dir
 
     with jax.named_scope("wait_right_hand_side"):
         left(flat)
         arrived(e_one)
     for X in range(10):
-        begin = coarse[0][1] * A[X]
+        begin = coarse[0][1] * A[X // 2, X % 2]
         XA[X] = begin
         CD[X] = begin
+
+    def of(ref):
+        return lambda X: ref[X]
+
     now, later = XA, XB
     for number in range(1, 4):
         for X in range(number, 10 - number):
-            later[X], CD[X] = coarse_step(now, CD, None, None, X, number)
+            later[X], CD[X] = coarse_step(of(now), of(CD), X, number)
         now, later = later, now
     for X in range(CX0, CX0 + 2):
-        new_x, new_d = coarse_step(now, CD, None, None, X, 4)
-        B[0, X, pl.ds(CR0, CRN), :] = new_x[CR0:CR0 + CRN]
-        B[1, X, pl.ds(CR0, CRN), :] = new_d[CR0:CR0 + CRN]
-    e_two = coarse_messages(B, (pl.ds(0, 2),), b_send, b_recv)
+        new_x, new_d = coarse_step(of(now), of(CD), X, 4)
+        B[2, ITERATE[X % 2], pl.ds(CR0, CRN), :] = new_x[CR0:CR0 + CRN]
+        B[2, STEP[X % 2], pl.ds(CR0, CRN), :] = new_d[CR0:CR0 + CRN]
+    e_two = coarse_messages(B, iterate_cut, b_send, b_recv)
     with jax.named_scope("wait_iterate"):
         left(coefs + e_one)
         arrived(late)
         left(late)
         arrived(e_two)
-    now, now_d = B.at[0], B.at[1]
+    iterate, step_of = (lambda X: B[X // 2, ITERATE[X % 2]]), (lambda X: B[X // 2, STEP[X % 2]])
     for number, later in ((5, XA), (6, XB), (7, XA)):
         for X in range(number - 4, 14 - number):
-            later[X], CD[X] = coarse_step(now, now_d, None, None, X, number)
-        now, now_d = later, CD
+            later[X], CD[X] = coarse_step(iterate, step_of, X, number)
+        iterate, step_of = of(later), of(CD)
 
     spread_z = jnp.where(
         lax.shift_right_logical(lax.broadcasted_iota(jnp.int32, (128, 256), 1), 1) == lax.broadcasted_iota(jnp.int32, (128, 256), 0),
@@ -404,7 +467,9 @@
     spread_y = jnp.where(
         lax.shift_right_logical(lax.broadcasted_iota(jnp.int32, (40, 24), 0) + (2 * CR0 - FR0), 1) == lax.broadcasted_iota(jnp.int32, (40, 24), 1),
         f32(1.0), f32(0.0))
-    corr = jnp.concatenate([C[3, X] * now[X] for X in range(3, 7)], 0)
+    crow = lax.broadcasted_iota(jnp.int32, (24, 128), 0)
+    in_rim = both(crow >= CR0 - 1, crow <= CR0 + CRN)
+    corr = jnp.concatenate([jnp.where(in_rim, coef(ROOT, X) * iterate(X), f32(0.0)) for X in range(3, 7)], 0)
     corr = dot(corr, spread_z)
     for X in range(4):
         fine_corr = dot(spread_y, corr[24 * X:24 * X + 24])
@@ -436,10 +501,10 @@
             vmem((4, 10, 2, 40, 128), jnp.float32),
             fine_slabs(), fine_slabs(), fine_slabs(), fine_slabs(), fine_slabs(),
             fine_slabs(), fine_slabs(), fine_slabs(), fine_slabs(), fine_slabs(),
-            vmem((4, 10, 24, 128), jnp.float32),
+            vmem((5, C_SLOTS, 24, 128), jnp.float32),
             vmem((3, 10, 24, 128), jnp.float32),
-            coarse_slabs(),
-            vmem((2, 10, 24, 128), jnp.float32),
+            vmem((5, A_SLOTS, 24, 128), jnp.float32),
+            vmem((5, B_SLOTS, 24, 128), jnp.float32),
             coarse_slabs(), coarse_slabs(), coarse_slabs(),
             dma((4, 2)),
             dma((n_rim,)), dma((n_rim,)),
@@ -447,7 +512,7 @@
             dma((n_near,)), dma((n_near,)),
             dma((n_near,)), dma((n_near,)),
             dma((n_ring,)), dma((n_ring,)),
-            pltpu.SemaphoreType.REGULAR((len(PLUS),)),
+            pltpu.SemaphoreType.REGULAR((len(NEAR),)),
         ],
         compiler_params=pltpu.CompilerParams(collective_id=0, has_side_effects=True, vmem_limit_bytes=48 * 2**20),
         name="cycle",

time: 32.6 us -> 31.3 us (0.960)
  Pallas kernels: 31.7 us -> 30.4 us
    pallas_call x1, Pallas kernels: 31.7 us -> 30.4 us  [body(): pl.pallas_call(kernel, out_shape=jax.ShapeDtypeStruct((4, 32, 256), jnp.f...]
where the time goes in v4:
time: 31.3 us; the launch traced here: 31.1 us
  Pallas kernels  30.4 us (97%)
  local copies, waits for them, and re-layouts  0.66 us (2%)
    pallas_call x1, Pallas kernels, body(): pl.pallas_call(kernel, out_shape=jax.ShapeDtypeStruct((4, 32, 256), jnp.f...  30.4 us
    unnamed x1, local copies, waits for them, and re-layouts  0.66 us

profile of v4, /device:TPU:1, one launch (start us, length us, event | category | flops | bytes accessed | tf_op | source)
XLA Modules:
  0.0 31.1 jit_solution(4134080404386298079)
XLA Ops:
  0.0 30.4 %cycle.1 = f32[4,32,256]{2,1,0:T(8,128)S(1)} custom-call(f32[4,32,256]{2,1,0:T(8,128)} %source.1, f32[4,32,256]{2,1,0:T(8,128)} %guess.1, f32[4,32,256]{2,1,0:T(8,128)} %mass.1, f32[4,32,256]{2,1,0:T(8,128)} %diff.1), custom_call_target="tpu_custom_call" | custom-call | tf_op jit(solution)/shard_map/cycle/pallas_call | solution.py:495
  30.4 0.7 %copy.6 = f32[4,32,256]{2,1,0:T(8,128)} copy(f32[4,32,256]{2,1,0:T(8,128)S(1)} %cycle.1) | data formatting | bytes 262144

commit v5 on v4

--- a/solution.py
+++ b/solution.py
@@ -19,7 +19,7 @@
 GUESS, DIFF, SOURCE, MASS = 0, 1, 2, 3
 
 NEAR = [(i, j) for i in (-2, 2, -1, 1) for j in (-1, 1)] + [(-2, 0), (2, 0), (0, -1), (0, 1), (-1, 0), (1, 0)]
-PLUS = [(0, 1), (1, -1), (1, 0), (1, 1), (2, -1), (2, 0), (2, 1)]
+BESIDE = [o for o in NEAR if abs(o[0]) < 2]
 LOW_Y, LOW_Z, LOW_X, ROOT = (0, 6), (1, 7), (2, 5), (3, 4)
 C_SLOTS, A_SLOTS, B_SLOTS = 8, 2, 4
 STEP, ITERATE = (0, 3), (1, 2)
@@ -90,7 +90,7 @@
     return jnp.dot(a, b, precision=lax.Precision.HIGHEST, preferred_element_type=jnp.float32)
 
 
-def kernel(source, guess, mass, diff, out, F, FX, FY, FZ, DIAG, INV, W1, W2, DIR, RES, L2, C, G, A, B, XA, XB, CD,
+def kernel(source, guess, mass, diff, out, F, FX, FY, FZ, DIAG, INV, W1, W2, DIR, RES, L2, C, G, A, B, XA, XB, CD, SPREAD,
            load_sem, r_send, r_recv, c_send, c_recv, e_send, e_recv, b_send, b_recv, l_send, l_recv, ready):
     f32 = jnp.float32
     nbox, nsub = lax.axis_size("box"), lax.axis_size("sub")
@@ -133,34 +133,34 @@
         return o, pltpu.make_async_remote_copy(
             src_ref=src, dst_ref=dst, send_sem=send, recv_sem=recv, device_id=(b + o[0], s + o[1]), device_id_type=MESH)
 
-    barrier = pltpu.get_barrier_semaphore()
-
-    def greet(o, semaphore):
-        pl.semaphore_signal(semaphore, inc=1, device_id=(b + o[0], s + o[1]), device_id_type=MESH)
-
-    def minus(o):
-        return (-o[0], -o[1])
-
-    origin = both(b == 0, s == 0)
-    other = jnp.logical_not(origin)
-
-    def is_origin(o):
-        return both(b + o[0] == 0, s + o[1] == 0)
-
-    def there(o):
-        return both(exists(o), jnp.logical_not(is_origin(o)))
-
-    MINUS = [minus(o) for o in PLUS]
-    for o in PLUS:
-        pl.when(both(exists(o), other))(functools.partial(greet, o, barrier))
-    for o in MINUS:
-        pl.when(is_origin(o))(functools.partial(greet, o, barrier))
     loads = []
     for k, ref in enumerate((guess, diff, source, mass)):
         for h in range(2):
             loads.append(pltpu.make_async_copy(
                 ref.at[:, :, pl.ds(128 * h, 128)], F.at[k, pl.ds(FX0, 4), h, pl.ds(FR0, FRN)], load_sem.at[k, h]))
             loads[-1].start()
+    barrier = pltpu.get_barrier_semaphore()
+
+    def greet(o, semaphore):
+        pl.semaphore_signal(semaphore, inc=1, device_id=(b + o[0], s + o[1]), device_id_type=MESH)
+
+    def minus(o):
+        return (-o[0], -o[1])
+
+    origin = both(b == 0, s == 0)
+    other = jnp.logical_not(origin)
+
+    def is_origin(o):
+        return both(b + o[0] == 0, s + o[1] == 0)
+
+    def there(o):
+        return both(exists(o), jnp.logical_not(is_origin(o)))
+
+    for o in BESIDE:
+        pl.when(both(exists(o), other))(functools.partial(greet, o, barrier))
+    for o in NEAR:
+        if abs(o[0]) == 2:
+            pl.when(is_origin(o))(functools.partial(greet, o, barrier))
     def outside(x_cut, row_cut, X_cut, coarse_row_cut, n_x, n_rows, n_X, n_coarse_rows):
         F[0:3, x_cut, :, row_cut] = jnp.zeros((3, n_x, 2, n_rows, 128), f32)
         F[3:4, x_cut, :, row_cut] = jnp.ones((1, n_x, 2, n_rows, 128), f32)
@@ -180,9 +180,6 @@
         pl.when(b == 1)(lambda: blank_coarse(slice(0, 1), every, 1, 24))
         pl.when(b == nbox - 2)(lambda: blank_coarse(slice(4, 5), every, 1, 24))
 
-    for load in loads:
-        load.wait()
-
     first, k = [], 0
     for group in rim_messages():
         first.append([])
@@ -191,24 +188,28 @@
             k += 1
     flat = [m for group in first for m in group]
     n_sub = jnp.minimum(s, 1) + jnp.minimum(nsub - 1 - s, 1)
-    n_minus = jnp.minimum(b, 2) * (n_sub + 1) + jnp.minimum(s, 1)
-    n_plus = jnp.minimum(nbox - 1 - b, 2) * (n_sub + 1) + jnp.minimum(nsub - 1 - s, 1)
-    by_origin = both(both(b < 3, s < 2), other)
+    n_beside = (jnp.minimum(b, 1) + jnp.minimum(nbox - 1 - b, 1) + 1) * (n_sub + 1) - 1
+    n_near = (jnp.minimum(b, 2) + jnp.minimum(nbox - 1 - b, 2) + 1) * (n_sub + 1) - 1
+    by_origin = both(both(b < 2, s < 2), other)
 
     def wait_barrier(count):
         pl.when(count > 0)(lambda: pl.semaphore_wait(barrier, count))
 
-    pl.when(origin)(lambda: wait_barrier(n_plus))
-    pl.when(by_origin)(lambda: wait_barrier(n_minus - 1))
-    pl.when(jnp.logical_not(jnp.logical_or(origin, by_origin)))(lambda: wait_barrier(n_minus))
+    pl.when(origin)(lambda: wait_barrier(n_near))
+    pl.when(by_origin)(lambda: wait_barrier(n_beside - 1))
+    pl.when(jnp.logical_not(jnp.logical_or(origin, by_origin)))(lambda: wait_barrier(n_beside))
 
     def slot(o):
         return ready.at[NEAR.index(o)]
 
-    for o in MINUS:
-        pl.when(there(o))(functools.partial(greet, o, slot(minus(o))))
-    for o in PLUS:
-        pl.when(both(exists(o), origin))(functools.partial(greet, o, slot(minus(o))))
+    @pl.when(origin)
+    def _():
+        for o in NEAR:
+            if o[0] >= 0 and o[1] >= 0:
+                pl.when(exists(o))(functools.partial(greet, o, slot(minus(o))))
+
+    for load in loads:
+        load.wait()
 
     def send(o):
         for m in flat:
@@ -219,14 +220,18 @@
         pl.semaphore_wait(slot(o), 1)
         send(o)
 
-    for o in MINUS[:4]:
-        pl.when(there(o))(functools.partial(send, o))
-    for o in PLUS[:4]:
-        pl.when(both(exists(o), origin))(functools.partial(send, o))
-    for o in PLUS[:4]:
-        pl.when(both(exists(o), other))(functools.partial(send_met, o))
-    for o in MINUS[:4]:
-        pl.when(is_origin(o))(functools.partial(send_met, o))
+    @pl.when(inner)
+    def _():
+        for _, m in flat:
+            m.start()
+
+    @pl.when(rim)
+    def _():
+        for o in BESIDE:
+            pl.when(there(o))(functools.partial(send, o))
+        for o in BESIDE:
+            if o[0] <= 0 and o[1] <= 0:
+                pl.when(is_origin(o))(functools.partial(send_met, o))
     pl.when(rim)(blank)
 
     lane = lax.broadcasted_iota(jnp.int32, (256, 128), 0)
@@ -311,41 +316,39 @@
 
     arrived(first[0])
     over(4, 7, face)
-    with jax.named_scope("rank_one"):
-        arrived(first[1])
-    with jax.named_scope("coarse_coefficients"):
-        def rows(ref, x, start):
-            return ref[x, :, pl.ds(start, 16, 2), :]
-
-        def wide(parts):
-            return jnp.concatenate([jnp.concatenate([v[0], v[1]], 1) for v in parts], 0)
-
-
-        D, M = F.at[DIFF], F.at[MASS]
-        pair = {x: rows(D, x, FR0) + rows(D, x, FR0 + 1) for x in range(FX0 - 1, FX1 + 1)}
-        low_y = {x: rows(D, x, FR0 - 1) + rows(D, x, FR0) for x in range(FX0, FX1)}
-        high_y = {x: rows(D, x, FR0 + 1) + rows(D, x, FR0 + 2) for x in range(FX0, FX1)}
-        in_mean, in_z = [], []
-        for X in range(2):
-            x = FX0 + 2 * X
-            face_low, face_high = 0.25 * (pair[x - 1] + pair[x]), 0.25 * (pair[x + 1] + pair[x + 2])
-            y_low, y_high = 0.25 * (low_y[x] + low_y[x + 1]), 0.25 * (high_y[x] + high_y[x + 1])
-            mean_mass = 0.25 * (rows(M, x, FR0) + rows(M, x, FR0 + 1) + rows(M, x + 1, FR0) + rows(M, x + 1, FR0 + 1))
-            in_mean += [face_low, y_low, mean_mass + 0.25 * (face_low + face_high + y_low + y_high)]
-            in_z.append(0.25 * (pair[x] + pair[x + 1]))
-        means = dot(wide(in_mean), z_mean)
-        over_z = wide(in_z)
-        lows_z, highs_z = dot(over_z, z_low), dot(over_z, z_high)
-        own_s = []
-        for X in range(2):
-            fx, fy, d = (means[(3 * X + k) * 16:(3 * X + k + 1) * 16] for k in range(3))
-            fz = lows_z[16 * X:16 * X + 16]
-            d = d + 0.25 * (fz + highs_z[16 * X:16 * X + 16])
-            sc = lax.rsqrt(d)
-            sc = sc * (1.5 - 0.5 * d * sc * sc)
-            own_s.append(sc)
-            for kind, v in ((LOW_X, fx), (LOW_Y, fy), (LOW_Z, fz), (ROOT, sc)):
-                C[2, kind[X], pl.ds(CR0, CRN), :] = v
+    arrived(first[1])
+    def rows(ref, x, start):
+        return ref[x, :, pl.ds(start, 16, 2), :]
+
+    def wide(parts):
+        return jnp.concatenate([jnp.concatenate([v[0], v[1]], 1) for v in parts], 0)
+
+
+    D, M = F.at[DIFF], F.at[MASS]
+    pair = {x: rows(D, x, FR0) + rows(D, x, FR0 + 1) for x in range(FX0 - 1, FX1 + 1)}
+    low_y = {x: rows(D, x, FR0 - 1) + rows(D, x, FR0) for x in range(FX0, FX1)}
+    high_y = {x: rows(D, x, FR0 + 1) + rows(D, x, FR0 + 2) for x in range(FX0, FX1)}
+    in_mean, in_z = [], []
+    for X in range(2):
+        x = FX0 + 2 * X
+        face_low, face_high = 0.25 * (pair[x - 1] + pair[x]), 0.25 * (pair[x + 1] + pair[x + 2])
+        y_low, y_high = 0.25 * (low_y[x] + low_y[x + 1]), 0.25 * (high_y[x] + high_y[x + 1])
+        mean_mass = 0.25 * (rows(M, x, FR0) + rows(M, x, FR0 + 1) + rows(M, x + 1, FR0) + rows(M, x + 1, FR0 + 1))
+        in_mean += [face_low, y_low, mean_mass + 0.25 * (face_low + face_high + y_low + y_high)]
+        in_z.append(0.25 * (pair[x] + pair[x + 1]))
+    means = dot(wide(in_mean), z_mean)
+    over_z = wide(in_z)
+    lows_z, highs_z = dot(over_z, z_low), dot(over_z, z_high)
+    own_s = []
+    for X in range(2):
+        fx, fy, d = (means[(3 * X + k) * 16:(3 * X + k + 1) * 16] for k in range(3))
+        fz = lows_z[16 * X:16 * X + 16]
+        d = d + 0.25 * (fz + highs_z[16 * X:16 * X + 16])
+        sc = lax.rsqrt(d)
+        sc = sc * (1.5 - 0.5 * d * sc * sc)
+        own_s.append(sc)
+        for kind, v in ((LOW_X, fx), (LOW_Y, fy), (LOW_Z, fz), (ROOT, sc)):
+            C[2, kind[X], pl.ds(CR0, CRN), :] = v
 
     def coarse_messages(src, cut, sends, recvs):
         found = []
@@ -360,28 +363,21 @@
     def meet(o):
         pl.semaphore_wait(slot(o), 1)
 
-    for o in PLUS[4:]:
-        pl.when(both(exists(o), other))(functools.partial(meet, o))
-    for o in MINUS[4:]:
+    for o in ((-2, 0), (-2, -1)):
         pl.when(is_origin(o))(functools.partial(meet, o))
     coefs = coarse_messages(C, coef_cut, c_send, c_recv)
 
-    with jax.named_scope("work_one"):
-        over(3, 8, face, 4)
-        over(3, 7, with_operator)
-    with jax.named_scope("rank_two"):
-        arrived(first[2])
-    with jax.named_scope("work_two"):
-        over(2, 9, face, 6)
-        over(2, 8, with_operator, 5)
-        over(3, 7, smooth)
-    with jax.named_scope("rank_three"):
-        arrived(first[3])
-    with jax.named_scope("work_three"):
-        over(1, 10, face, 8)
-        over(1, 9, with_operator, 7)
-        over(2, 8, smooth, 5)
-        over(FX0, FX1, find_residual)
+    over(3, 8, face, 4)
+    over(3, 7, with_operator)
+    arrived(first[2])
+    over(2, 9, face, 6)
+    over(2, 8, with_operator, 5)
+    over(3, 7, smooth)
+    arrived(first[3])
+    over(1, 10, face, 8)
+    over(1, 9, with_operator, 7)
+    over(2, 8, smooth, 5)
+    over(FX0, FX1, find_residual)
 
     means = []
     for X in range(2):
@@ -405,8 +401,7 @@
         late.append(message(o, L2.at[xs, :, rs], L2.at[xd, :, rd], l_send.at[k], l_recv.at[k]))
     start(late)
 
-    with jax.named_scope("wait_coefficients"):
-        arrived(coefs)
+    arrived(coefs)
     clane = lax.broadcasted_iota(jnp.int32, (24, 128), 1)
 
     def coef(kind, X):
@@ -429,9 +424,8 @@
         step_dir = keep * step_of(X) + gain * c
         return x + step_dir, step_dir
 
-    with jax.named_scope("wait_right_hand_side"):
-        left(flat)
-        arrived(e_one)
+    left(flat)
+    arrived(e_one)
     for X in range(10):
         begin = coarse[0][1] * A[X // 2, X % 2]
         XA[X] = begin
@@ -450,11 +444,10 @@
         B[2, ITERATE[X % 2], pl.ds(CR0, CRN), :] = new_x[CR0:CR0 + CRN]
         B[2, STEP[X % 2], pl.ds(CR0, CRN), :] = new_d[CR0:CR0 + CRN]
     e_two = coarse_messages(B, iterate_cut, b_send, b_recv)
-    with jax.named_scope("wait_iterate"):
-        left(coefs + e_one)
-        arrived(late)
-        left(late)
-        arrived(e_two)
+    left(coefs + e_one)
+    arrived(late)
+    left(late)
+    arrived(e_two)
     iterate, step_of = (lambda X: B[X // 2, ITERATE[X % 2]]), (lambda X: B[X // 2, STEP[X % 2]])
     for number, later in ((5, XA), (6, XB), (7, XA)):
         for X in range(number - 4, 14 - number):
@@ -464,18 +457,14 @@
     spread_z = jnp.where(
         lax.shift_right_logical(lax.broadcasted_iota(jnp.int32, (128, 256), 1), 1) == lax.broadcasted_iota(jnp.int32, (128, 256), 0),
         f32(1.0), f32(0.0))
-    spread_y = jnp.where(
-        lax.shift_right_logical(lax.broadcasted_iota(jnp.int32, (40, 24), 0) + (2 * CR0 - FR0), 1) == lax.broadcasted_iota(jnp.int32, (40, 24), 1),
-        f32(1.0), f32(0.0))
-    crow = lax.broadcasted_iota(jnp.int32, (24, 128), 0)
-    in_rim = both(crow >= CR0 - 1, crow <= CR0 + CRN)
-    corr = jnp.concatenate([jnp.where(in_rim, coef(ROOT, X) * iterate(X), f32(0.0)) for X in range(3, 7)], 0)
-    corr = dot(corr, spread_z)
+    corr = dot(jnp.concatenate([coef(ROOT, X) * iterate(X) for X in range(3, 7)], 0), spread_z)
     for X in range(4):
-        fine_corr = dot(spread_y, corr[24 * X:24 * X + 24])
-        fine_corr = jnp.stack([fine_corr[:, :128], fine_corr[:, 128:]])
-        for x in (2 * X + 1, 2 * X + 2):
-            W2[x] = L2[x] + fine_corr
+        for h in range(2):
+            part = corr[24 * X:24 * X + 24, 128 * h:128 * h + 128]
+            SPREAD[X, h, pl.ds(0, 24, 2), :] = part
+            SPREAD[X, h, pl.ds(1, 24, 2), :] = part
+    for x in range(1, 9):
+        W2[x] = L2[x] + SPREAD[(x - 1) // 2, :, pl.ds(2 * CR0 - FR0, 40), :]
 
     over(2, 8, functools.partial(first_step, W2, W1))
     for x in range(FX0, FX1):
@@ -506,6 +495,7 @@
             vmem((5, A_SLOTS, 24, 128), jnp.float32),
             vmem((5, B_SLOTS, 24, 128), jnp.float32),
             coarse_slabs(), coarse_slabs(), coarse_slabs(),
+            vmem((4, 2, 48, 128), jnp.float32),
             dma((4, 2)),
             dma((n_rim,)), dma((n_rim,)),
             dma((n_near,)), dma((n_near,)),

time: 31.3 us -> 30.5 us (0.974)
  Pallas kernels: 30.4 us -> 29.6 us
    pallas_call x1, Pallas kernels: 30.4 us -> 29.6 us  [body(): pl.pallas_call(kernel, out_shape=jax.ShapeDtypeStruct((4, 32, 256), jnp.f...]
where the time goes in v5:
time: 30.5 us; the launch traced here: 30.3 us
  Pallas kernels  29.6 us (97%)
  local copies, waits for them, and re-layouts  0.66 us (2%)
    pallas_call x1, Pallas kernels, body(): pl.pallas_call(kernel, out_shape=jax.ShapeDtypeStruct((4, 32, 256), jnp.f...  29.6 us
    unnamed x1, local copies, waits for them, and re-layouts  0.66 us

profile of v5, /device:TPU:1, one launch (start us, length us, event | category | flops | bytes accessed | tf_op | source)
XLA Modules:
  0.0 30.3 jit_solution(8713336622900114648)
XLA Ops:
  0.0 29.6 %cycle.1 = f32[4,32,256]{2,1,0:T(8,128)S(1)} custom-call(f32[4,32,256]{2,1,0:T(8,128)} %source.1, f32[4,32,256]{2,1,0:T(8,128)} %guess.1, f32[4,32,256]{2,1,0:T(8,128)} %mass.1, f32[4,32,256]{2,1,0:T(8,128)} %diff.1), custom_call_target="tpu_custom_call" | custom-call | tf_op jit(solution)/shard_map/cycle/pallas_call | solution.py:484
  29.6 0.7 %copy.6 = f32[4,32,256]{2,1,0:T(8,128)} copy(f32[4,32,256]{2,1,0:T(8,128)S(1)} %cycle.1) | data formatting | bytes 262144

commit v6 on v5

--- a/solution.py
+++ b/solution.py
@@ -87,7 +87,14 @@
 
 
 def dot(a, b):
-    return jnp.dot(a, b, precision=lax.Precision.HIGHEST, preferred_element_type=jnp.float32)
+    bf16 = jnp.bfloat16
+    high = a.astype(bf16)
+    rest = a - high.astype(jnp.float32)
+    middle = rest.astype(bf16)
+    low = (rest - middle.astype(jnp.float32)).astype(bf16)
+    parts = jnp.dot(jnp.concatenate([low, middle, high], 0), b.astype(bf16), preferred_element_type=jnp.float32)
+    n = a.shape[0]
+    return (parts[:n] + parts[n:2 * n]) + parts[2 * n:]
 
 
 def kernel(source, guess, mass, diff, out, F, FX, FY, FZ, DIAG, INV, W1, W2, DIR, RES, L2, C, G, A, B, XA, XB, CD, SPREAD,
@@ -133,29 +140,46 @@
         return o, pltpu.make_async_remote_copy(
             src_ref=src, dst_ref=dst, send_sem=send, recv_sem=recv, device_id=(b + o[0], s + o[1]), device_id_type=MESH)
 
+    barrier = pltpu.get_barrier_semaphore()
+
+    def greet(o, semaphore):
+        pl.semaphore_signal(semaphore, inc=1, device_id=(b + o[0], s + o[1]), device_id_type=MESH)
+
+    def minus(o):
+        return (-o[0], -o[1])
+
+    origin = both(b == 0, s == 0)
+    other = jnp.logical_not(origin)
+
+    def is_origin(o):
+        return both(b + o[0] == 0, s + o[1] == 0)
+
+    def there(o):
+        return both(exists(o), jnp.logical_not(is_origin(o)))
+
+    n_sub = jnp.minimum(s, 1) + jnp.minimum(nsub - 1 - s, 1)
+    n_beside = (jnp.minimum(b, 1) + jnp.minimum(nbox - 1 - b, 1) + 1) * (n_sub + 1) - 1
+    n_near = (jnp.minimum(b, 2) + jnp.minimum(nbox - 1 - b, 2) + 1) * (n_sub + 1) - 1
+
+    def wait_barrier(count):
+        pl.when(count > 0)(lambda: pl.semaphore_wait(barrier, count))
+
+    def slot(o):
+        return ready.at[NEAR.index(o)]
+
+    @pl.when(origin)
+    def _():
+        wait_barrier(n_near)
+        for o in NEAR:
+            if o[0] >= 0 and o[1] >= 0:
+                pl.when(exists(o))(functools.partial(greet, o, slot(minus(o))))
+
     loads = []
     for k, ref in enumerate((guess, diff, source, mass)):
         for h in range(2):
             loads.append(pltpu.make_async_copy(
                 ref.at[:, :, pl.ds(128 * h, 128)], F.at[k, pl.ds(FX0, 4), h, pl.ds(FR0, FRN)], load_sem.at[k, h]))
             loads[-1].start()
-    barrier = pltpu.get_barrier_semaphore()
-
-    def greet(o, semaphore):
-        pl.semaphore_signal(semaphore, inc=1, device_id=(b + o[0], s + o[1]), device_id_type=MESH)
-
-    def minus(o):
-        return (-o[0], -o[1])
-
-    origin = both(b == 0, s == 0)
-    other = jnp.logical_not(origin)
-
-    def is_origin(o):
-        return both(b + o[0] == 0, s + o[1] == 0)
-
-    def there(o):
-        return both(exists(o), jnp.logical_not(is_origin(o)))
-
     for o in BESIDE:
         pl.when(both(exists(o), other))(functools.partial(greet, o, barrier))
     for o in NEAR:
@@ -187,26 +211,10 @@
             first[-1].append(message(o, F.at[arrays, xs, :, rs], F.at[arrays, xd, :, rd], r_send.at[k], r_recv.at[k]))
             k += 1
     flat = [m for group in first for m in group]
-    n_sub = jnp.minimum(s, 1) + jnp.minimum(nsub - 1 - s, 1)
-    n_beside = (jnp.minimum(b, 1) + jnp.minimum(nbox - 1 - b, 1) + 1) * (n_sub + 1) - 1
-    n_near = (jnp.minimum(b, 2) + jnp.minimum(nbox - 1 - b, 2) + 1) * (n_sub + 1) - 1
     by_origin = both(both(b < 2, s < 2), other)
 
-    def wait_barrier(count):
-        pl.when(count > 0)(lambda: pl.semaphore_wait(barrier, count))
-
-    pl.when(origin)(lambda: wait_barrier(n_near))
     pl.when(by_origin)(lambda: wait_barrier(n_beside - 1))
     pl.when(jnp.logical_not(jnp.logical_or(origin, by_origin)))(lambda: wait_barrier(n_beside))
-
-    def slot(o):
-        return ready.at[NEAR.index(o)]
-
-    @pl.when(origin)
-    def _():
-        for o in NEAR:
-            if o[0] >= 0 and o[1] >= 0:
-                pl.when(exists(o))(functools.partial(greet, o, slot(minus(o))))
 
     for load in loads:
         load.wait()
@@ -447,6 +455,7 @@
     left(coefs + e_one)
     arrived(late)
     left(late)
+    left(e_two)
     arrived(e_two)
     iterate, step_of = (lambda X: B[X // 2, ITERATE[X % 2]]), (lambda X: B[X // 2, STEP[X % 2]])
     for number, later in ((5, XA), (6, XB), (7, XA)):
@@ -471,8 +480,6 @@
         last = second_step(x)
         for h in range(2):
             out[x - FX0, :, 128 * h:128 * h + 128] = last[h, FR0:FR0 + FRN]
-
-    left(e_two)
 
 
 def body(source, guess, mass_coef, diffusion):

time: 30.5 us -> 30.2 us (level)
  no operation moved by 1% of the time
where the time goes in v6:
time: 30.2 us; the launch traced here: 30 us
  Pallas kernels  29.4 us (97%)
  local copies, waits for them, and re-layouts  0.66 us (2%)
    pallas_call x1, Pallas kernels, body(): pl.pallas_call(kernel, out_shape=jax.ShapeDtypeStruct((4, 32, 256), jnp.f...  29.4 us
    unnamed x1, local copies, waits for them, and re-layouts  0.66 us

profile of v6, /device:TPU:1, one launch (start us, length us, event | category | flops | bytes accessed | tf_op | source)
XLA Modules:
  0.0 30.0 jit_solution(8262404705913541327)
XLA Ops:
  0.0 29.4 %cycle.1 = f32[4,32,256]{2,1,0:T(8,128)S(1)} custom-call(f32[4,32,256]{2,1,0:T(8,128)} %source.1, f32[4,32,256]{2,1,0:T(8,128)} %guess.1, f32[4,32,256]{2,1,0:T(8,128)} %mass.1, f32[4,32,256]{2,1,0:T(8,128)} %diff.1), custom_call_target="tpu_custom_call" | custom-call | tf_op jit(solution)/shard_map/cycle/pallas_call | solution.py:491
  29.4 0.7 %copy.6 = f32[4,32,256]{2,1,0:T(8,128)} copy(f32[4,32,256]{2,1,0:T(8,128)S(1)} %cycle.1) | data formatting | bytes 262144

commit v7 on v6

--- a/solution.py
+++ b/solution.py
@@ -18,7 +18,7 @@
 CX0, CR0, CRN = 4, 4, 16
 GUESS, DIFF, SOURCE, MASS = 0, 1, 2, 3
 
-NEAR = [(i, j) for i in (-2, 2, -1, 1) for j in (-1, 1)] + [(-2, 0), (2, 0), (0, -1), (0, 1), (-1, 0), (1, 0)]
+NEAR = [(i, j) for i in (-2, 2) for j in (-1, 1, 0)] + [(i, j) for i in (-1, 1) for j in (-1, 1)] + [(0, -1), (0, 1), (-1, 0), (1, 0)]
 BESIDE = [o for o in NEAR if abs(o[0]) < 2]
 LOW_Y, LOW_Z, LOW_X, ROOT = (0, 6), (1, 7), (2, 5), (3, 4)
 C_SLOTS, A_SLOTS, B_SLOTS = 8, 2, 4
@@ -419,16 +419,18 @@
         sc = coef(ROOT, X)
         G[0, X] = coef(LOW_X, X) * ((0.25 * sc) * coef(ROOT, X - 1))
         if X < 9:
-            G[1, X] = coef(LOW_Y, X) * ((0.25 * sc) * pltpu.roll(sc, 1, 0))
-            G[2, X] = jnp.where(clane == 0, f32(0.0), coef(LOW_Z, X) * ((0.25 * sc) * pltpu.roll(sc, 1, 1)))
+            low_row = coef(LOW_Y, X) * ((0.25 * sc) * pltpu.roll(sc, 1, 0))
+            low_lane = jnp.where(clane == 0, f32(0.0), coef(LOW_Z, X) * ((0.25 * sc) * pltpu.roll(sc, 1, 1)))
+            G[1, X], G[2, X] = low_row, low_lane
+            G[3, X], G[4, X] = pltpu.roll(low_row, 23, 0), pltpu.roll(low_lane, 127, 1)
 
     def coarse_step(iterate, step_of, X, number):
         keep, gain = coarse[number]
         x = iterate(X)
-        gy, gz = G[1, X], G[2, X]
         c = (A[X // 2, X % 2] - x) + G[0, X] * iterate(X - 1) + G[0, X + 1] * iterate(X + 1)
-        c = c + gy * pltpu.roll(x, 1, 0) + pltpu.roll(gy * x, 23, 0)
-        c = c + gz * pltpu.roll(x, 1, 1) + pltpu.roll(gz * x, 127, 1)
+        along_y = G[1, X] * pltpu.roll(x, 1, 0) + G[3, X] * pltpu.roll(x, 23, 0)
+        along_z = G[2, X] * pltpu.roll(x, 1, 1) + G[4, X] * pltpu.roll(x, 127, 1)
+        c = c + (along_y + along_z)
         step_dir = keep * step_of(X) + gain * c
         return x + step_dir, step_dir
 
@@ -498,7 +500,7 @@
             fine_slabs(), fine_slabs(), fine_slabs(), fine_slabs(), fine_slabs(),
             fine_slabs(), fine_slabs(), fine_slabs(), fine_slabs(), fine_slabs(),
             vmem((5, C_SLOTS, 24, 128), jnp.float32),
-            vmem((3, 10, 24, 128), jnp.float32),
+            vmem((5, 10, 24, 128), jnp.float32),
             vmem((5, A_SLOTS, 24, 128), jnp.float32),
             vmem((5, B_SLOTS, 24, 128), jnp.float32),
             coarse_slabs(), coarse_slabs(), coarse_slabs(),

time: 30.2 us -> 30.1 us (level)
  no operation moved by 1% of the time
where the time goes in v7:
time: 30.1 us; the launch traced here: 29.9 us
  Pallas kernels  29.2 us (97%)
  local copies, waits for them, and re-layouts  0.66 us (2%)
    pallas_call x1, Pallas kernels, body(): pl.pallas_call(kernel, out_shape=jax.ShapeDtypeStruct((4, 32, 256), jnp.f...  29.2 us
    unnamed x1, local copies, waits for them, and re-layouts  0.66 us

profile of v7, /device:TPU:1, one launch (start us, length us, event | category | flops | bytes accessed | tf_op | source)
XLA Modules:
  0.0 29.9 jit_solution(5584900891145260695)
XLA Ops:
  0.0 29.2 %cycle.1 = f32[4,32,256]{2,1,0:T(8,128)S(1)} custom-call(f32[4,32,256]{2,1,0:T(8,128)} %source.1, f32[4,32,256]{2,1,0:T(8,128)} %guess.1, f32[4,32,256]{2,1,0:T(8,128)} %mass.1, f32[4,32,256]{2,1,0:T(8,128)} %diff.1), custom_call_target="tpu_custom_call" | custom-call | tf_op jit(solution)/shard_map/cycle/pallas_call | solution.py:493
  29.2 0.7 %copy.6 = f32[4,32,256]{2,1,0:T(8,128)} copy(f32[4,32,256]{2,1,0:T(8,128)S(1)} %cycle.1) | data formatting | bytes 262144
